TPU v7x, 512 devices: a whole 4x4x16 slice. The times are simulated.
512 devices in a mesh: row: 32 (over y_hi, z), col: 16 (over y_lo, x, core).
Axes of the slice: x: 4, y: 4 (y_hi: 2, y_lo: 2; y = y_hi * 2 + y_lo), z: 16, core: 2. Of those that a mesh axis runs over, the one named last changes fastest.
Arguments:
- features: bfloat16 [16, 1024, 256], P('col', 'row'), may hold values from -6 to 6
- node_order: int32 [16, 1024], P('col'), may hold values from 0 to 1023, each once within a row
- tile_weights: bfloat16 [16384, 128, 128], P(('row', 'col')), may hold values from 0 to 4, as said below
- tile_rows: int32 [16384], P(('row', 'col')), may hold values from 0 to 7, as said below
- tile_cols: int32 [16384], P(('row', 'col')), may hold values from 0 to 7
- tile_count: int32 [512], P(('row', 'col')), may hold values from 8 to 32, as said below
- weight: bfloat16 [256, 256], replicated, may hold values from -0.375 to 0.375
- bias_vector: float32 [256], replicated, may hold values from -3 to 3
- cotangent: bfloat16 [32768, 256], P(('row', 'col')), may hold values from -6 to 6
Outputs:
- output: bfloat16 [32768, 256], P(('row', 'col'))
- feature_grad: bfloat16 [16, 1024, 256], P('col', 'row')
- weight_grad: float32 [256, 256], replicated
- bias_grad: float32 [256], replicated
Inputs may be any that keep to these rules, and one draw needn't show every extreme that they name: Device block b (row index times 16 plus column index) uses slots 0 to tile_count[b] - 1 of its 32; later slots are ignored. At least one device uses all 32 slots. `tile_weights`: every entry is a whole number. `tile_rows`: in a row block, up to two of its 8 destination tiles (never all) may be named by no slot of any of its devices; at least one row block leaves one or more tiles out.
All inputs are finite; a program needn't handle non-finite values.
Results may differ from a plain program's by a relative error of at most 0.0075.
Values may be sent and summed in bfloat16 or wider, within the bound.
No kernel may reach another device: no remote copies, remote signals or barrier semaphores. Data moves between devices by JAX's collectives and lax.ppermute only.
A program may use at most 64 MiB of HBM per device.

v0:
```python
import jax
import jax.numpy as jnp
from jax import lax
from jax.sharding import PartitionSpec as P

DEST_TILES = 8
ST = 8


def silu_slope(values):
    sigma = jax.nn.sigmoid(values)
    return sigma * (1.0 + values * (1.0 - sigma))


def tile_products(
    edge_tiles, chosen_index, target_index, source_tiles, out_tiles, live_count, transposed
):
    tile_size = source_tiles.shape[1]
    feat_width = source_tiles.shape[2]
    group_size = 8
    num_turns = (live_count + group_size - 1) // group_size

    def one_turn(turn_index, running):
        start_slot = turn_index * group_size
        edge_group = lax.dynamic_slice_in_dim(edge_tiles, start_slot, group_size, 0)
        pick_group = lax.dynamic_slice_in_dim(chosen_index, start_slot, group_size, 0)
        place_group = lax.dynamic_slice_in_dim(target_index, start_slot, group_size, 0)
        tile_inputs = source_tiles[pick_group]
        if transposed:
            products = jnp.einsum(
                "kij,kif->kjf", edge_group, tile_inputs, preferred_element_type=jnp.float32
            )
        else:
            products = jnp.einsum(
                "kij,kjf->kif", edge_group, tile_inputs, preferred_element_type=jnp.float32
            )
        selector = (jnp.arange(out_tiles, dtype=jnp.int32)[:, None] == place_group[None, :]).astype(
            jnp.float32
        )
        return running + jnp.einsum(
            "dk,kif->dif", selector, products, precision=lax.Precision.HIGHEST
        )

    start_value = jnp.zeros((out_tiles, tile_size, feat_width), jnp.float32)
    return lax.fori_loop(0, num_turns, one_turn, start_value)


def body(
    features,
    node_order,
    tile_weights,
    tile_rows,
    tile_cols,
    tile_count,
    weight,
    bias_vector,
    cotangent,
):
    tile_size = tile_weights.shape[1]
    feat_width = features.shape[2]
    slot_total = tile_weights.shape[0]
    live_count = tile_count[0]
    live_slots = jnp.arange(slot_total, dtype=jnp.int32) < live_count
    edge_tiles = jnp.where(live_slots[:, None, None], tile_weights, jnp.zeros_like(tile_weights))
    gathered = lax.all_gather(features, "row", axis=1, tiled=True)[0]
    ordered = gathered[node_order[0]]
    src_tiles = ordered.reshape(ST, tile_size, feat_width)
    tile_sums = tile_products(
        edge_tiles, tile_cols, tile_rows, src_tiles, DEST_TILES, live_count, False
    )
    selector = (jnp.arange(DEST_TILES, dtype=jnp.int32)[:, None] == tile_rows[None, :]).astype(
        jnp.float32
    )
    row_weights = jnp.sum(edge_tiles, axis=2, dtype=jnp.float32)
    degree = jnp.einsum("dk,ki->di", selector, row_weights, precision=lax.Precision.HIGHEST)
    partial_sums = tile_sums.reshape(DEST_TILES * tile_size, feat_width)
    degree = degree.reshape(DEST_TILES * tile_size)
    own_sums, own_degree = (
        lax.psum_scatter(partial_sums, "col", scatter_dimension=0, tiled=True),
        lax.psum_scatter(degree, "col", scatter_dimension=0, tiled=True),
    )
    row_scale = lax.rsqrt(jnp.maximum(own_degree, 1.0))
    own_agg = (own_sums * row_scale[:, None]).astype(jnp.bfloat16)
    own_pre = jnp.dot(own_agg, weight, preferred_element_type=jnp.float32) + bias_vector
    own_grad = (cotangent.astype(jnp.float32) * silu_slope(own_pre)).astype(jnp.bfloat16)
    own_dsum = (
        jnp.dot(own_grad, weight.T, preferred_element_type=jnp.float32) * row_scale[:, None]
    ).astype(jnp.bfloat16)
    grad_sums = lax.all_gather(own_dsum, "col", axis=0, tiled=True)
    output = jax.nn.silu(own_pre).astype(jnp.bfloat16)
    weight_term = jnp.dot(own_agg.T, own_grad, preferred_element_type=jnp.float32)
    bias_term = jnp.sum(own_grad.astype(jnp.float32), axis=0)
    weight_grad, bias_grad = lax.psum((weight_term, bias_term), ("row", "col"))
    grad_tiles = grad_sums.reshape(DEST_TILES, tile_size, feat_width)
    src_grads = tile_products(edge_tiles, tile_rows, tile_cols, grad_tiles, ST, live_count, True)
    restored = (
        jnp.zeros((ST * tile_size, feat_width), jnp.float32)
        .at[node_order[0]]
        .set(src_grads.reshape(ST * tile_size, feat_width))
    )
    own_source = lax.psum_scatter(restored, "row", scatter_dimension=0, tiled=True)
    feature_grad = own_source.astype(jnp.bfloat16)[None]
    return (output, feature_grad, weight_grad, bias_grad)


def solution(mesh):
    return jax.shard_map(
        body,
        mesh=mesh,
        in_specs=(
            P("col", "row", None),
            P("col", None),
            P(("row", "col"), None, None),
            P(("row", "col")),
            P(("row", "col")),
            P(("row", "col")),
            P(),
            P(),
            P(("row", "col"), None),
        ),
        out_specs=(P(("row", "col"), None), P("col", "row", None), P(), P()),
        check_vma=False,
    )
```

profile of v0, /device:TPU:1, one launch (start us, length us, event | category | flops | bytes accessed | tf_op | source)
XLA Modules:
  0.0 1312.9 jit_solution(8554924395056138116)
XLA Ops:
  7.2 0.0 copy-start
  7.2 0.0 reduce-scatter.3.cloned.1.call-start
  7.9 0.0 copy-start.2
  7.9 0.0 copy-start.3
  7.9 1.6 copy.19
  9.6 72.4 %all_gather.6 = bf16[1,1024,256]{2,1,0:T(8,128)(2,1)S(1)} all-gather(bf16[1,32,256]{2,1,0:T(8,128)(2,1)S(1)} %copy-done.2), channel_id=1, replica_groups=mesh['row'=32,'col'=16] {'row'}, dimensions={1}, use_global_device_ids=true | all-gather | bytes 540672 | tf_op jit(solution)/shard_map/all_gather | solution.py:65
  82.0 0.4 convert_reduce_fusion
  82.4 3.9 gather_fusion.2
  86.4 0.0 copy-start.4
  86.4 0.0 copy-start.7
  86.4 0.1 broadcast.48.clone
  86.5 0.6 copy-done.4
  87.0 0.0 copy-done.7
  87.0 2.4 while.20
  87.0 0.1 compare_select_fusion.5
  87.1 0.6 gather_fusion
  87.7 0.4 fusion.41
  88.1 0.1 dynamic_slice.32
  88.1 1.3 convolution_add_fusion.5
  89.5 1.3 copy.21
  90.8 0.0 reduce-scatter.3.cloned.1.call-update
  90.8 0.0 reduce-scatter.5.cloned.1.call-start
  90.9 1.3 dynamic-slice
  92.8 0.1 convolution_bitcast_fusion
  92.9 42.9 %all-reduce = f32[1024]{0:T(1024)S(1)} all-reduce(f32[1024]{0:T(1024)S(1)} %convolution_bitcast_fusion), channel_id=3, replica_groups=mesh['row'=32,'col'=16] {'col'}, use_global_device_ids=true, to_apply=%region_4.5.clone | all-reduce | flops 1024 | bytes 8192
  135.8 0.1 fusion.18
  135.9 31.7 %reduce-scatter.3.cloned.1.call-done = f32[64,256]{1,0:T(8,128)} async-done(((f32[1024,256]{1,0:T(8,128)}), f32[64,256]{1,0:T(8,128)}) %reduce-scatter.3.cloned.1.call-update) | async-done | bytes 65552 | tf_op jit(solution)/shard_map/reduce_scatter | solution.py:79
  167.6 1.7 convert_reduce_fusion.1
  169.3 0.2 fusion.14
  169.5 20.7 %all_gather.7 = bf16[1024,256]{1,0:T(8,128)(2,1)S(1)} all-gather(bf16[64,256]{1,0:T(8,128)(2,1)S(1)} %fusion.14), channel_id=1, replica_groups=mesh['row'=32,'col'=16] {'col'}, dimensions={0}, use_global_device_ids=true | all-gather | bytes 557056 | tf_op jit(solution)/shard_map/all_gather | solution.py:89
  190.1 0.1 broadcast.48
  190.2 2.4 while.21
  190.2 0.1 compare_select_fusion.6
  190.3 0.6 gather_fusion.1
  190.9 0.3 fusion.46
  191.2 0.1 dynamic_slice.35
  191.3 1.3 convolution_add_fusion.6
  192.6 0.3 copy.22
  193.0 5.8 scatter_custom_fusion
  198.8 0.0 reduce-scatter.5.cloned.1.call-update
  198.8 0.0 all-reduce.3.cloned.1.call-start
  198.8 109.8 %psum.15 = f32[256]{0:T(256)} all-reduce(f32[256]{0:T(256)S(1)} %get-tuple-element.117), channel_id=1, replica_groups=mesh['row'=32,'col'=16] {'row','col'}, use_global_device_ids=true, to_apply=%region_11.12 | all-reduce | flops 256 | bytes 2048 | tf_op jit(solution)/shard_map/psum | solution.py:93
  308.6 1.0 fusion.19
  309.6 0.0 all-reduce.3.cloned.1.call-update
  309.6 524.5 %reduce-scatter.5.cloned.1.call-done = f32[32,256]{1,0:T(8,128)} async-done(((f32[1024,256]{1,0:T(8,128)}), f32[32,256]{1,0:T(8,128)}) %reduce-scatter.5.cloned.1.call-update) | async-done | bytes 32784 | tf_op jit(solution)/shard_map/reduce_scatter | solution.py:101
  834.1 1.4 convert_bitcast_fusion
  835.5 469.2 %all-reduce.3.cloned.1.call-done = f32[256,256]{1,0:T(8,128)} async-done(((f32[256,256]{1,0:T(8,128)}), f32[256,256]{1,0:T(8,128)}) %all-reduce.3.cloned.1.call-update) | async-done | bytes 262160 | tf_op jit(solution)/shard_map/psum | solution.py:93
  1304.7 1.7 copy.47
  (14 shorter events, 0.1 us)
Async XLA Ops:
  7.2 160.4 %copy-start = (bf16[256,256]{1,0:T(8,128)(2,1)S(1)}, bf16[256,256]{1,0:T(8,128)(2,1)}, u32[]{:S(2)}) copy-start(bf16[256,256]{1,0:T(8,128)(2,1)} %param.19) | copy-start | bytes 393220
  7.2 160.4 %reduce-scatter.3.cloned.1.call-start = ((), (), s32[]{:S(2)}) async-start(), calls=%async_computation.2 | async-start | bytes 1114112 | tf_op jit(solution)/shard_map/reduce_scatter | solution.py:79
  7.9 1.7 copy-start.2
  7.9 74.1 %copy-start.3 = (s32[1,1024]{1,0:T(1,128)S(1)}, s32[1,1024]{1,0:T(1,128)}, u32[]{:S(2)}) copy-start(s32[1,1024]{1,0:T(1,128)} %param.14) | copy-start | bytes 12292
  86.4 0.7 copy-start.4
  86.4 0.7 copy-start.7
  90.8 76.8 %copy-start.5 = (bf16[64,256]{1,0:T(8,128)(2,1)S(1)}, bf16[64,256]{1,0:T(8,128)(2,1)}, u32[]{:S(2)}) copy-start(bf16[64,256]{1,0:T(8,128)(2,1)} %param.21) | copy-start | bytes 98308
  90.8 76.8 %copy-start.6 = (f32[256]{0:T(256)S(1)}, f32[256]{0:T(256)}, u32[]{:S(2)}) copy-start(f32[256]{0:T(256)} %param.20) | copy-start | bytes 3076
  90.8 743.3 %reduce-scatter.5.cloned.1.call-start = ((), (), s32[]{:S(2)}) async-start(), calls=%async_computation.3 | async-start | bytes 1081344 | tf_op jit(solution)/shard_map/reduce_scatter | solution.py:101
  193.0 115.6 %copy-start.1 = (f32[64,256]{1,0:T(8,128)S(1)}, f32[64,256]{1,0:T(8,128)}, u32[]{:S(2)}) copy-start(f32[64,256]{1,0:T(8,128)} %reduce-scatter.3.cloned.1.call-done) | copy-start | bytes 196612
  198.8 1105.9 %all-reduce.3.cloned.1.call-start = ((), (), s32[]{:S(2)}) async-start(), calls=%async_computation.4 | async-start | bytes 524288 | tf_op jit(solution)/shard_map/psum | solution.py:93
Sparse Core Ops, SparseCore 0:
  90.9 76.6 reduce-scatter.2
  198.9 635.1 reduce-scatter.4
  840.2 464.5 all-reduce.2
where the time goes:
time: 1310 us
  waiting for transfers between devices  1030 us (79%)
  blocking collectives  246 us (19%)
  local copies, waits for them, and re-layouts  18 us (1%)
  between operations  15.2 us (1%)
    reduce_scatter x1, waiting for transfers between devices, body(): lax.psum_scatter(restored, 'row', scatter_dimension=0, tiled=True)  525 us
    psum x1, waiting for transfers between devices, body(): weight_grad, bias_grad = lax.psum((weight_term, bias_term), ('row', 'col'))  469 us
    psum x1, blocking collectives, body(): weight_grad, bias_grad = lax.psum((weight_term, bias_term), ('row', 'col'))  110 us
    all_gather x1, blocking collectives, body(): gathered = lax.all_gather(features, 'row', axis=1, tiled=True)[0]  72.4 us
    unnamed x1, blocking collectives  42.9 us
    reduce_scatter x1, waiting for transfers between devices, body(): lax.psum_scatter(partial_sums, 'col', scatter_dimension=0, tiled=True)  31.7 us
  transfers between devices with their start and end apart: 3, of which 3 were waited for; matrix products, arithmetic and copies ran while one was open for 0% of the time, Pallas kernels for 0%

commit v1 on v0

v1 whole, which is shorter than its diff:
```python
import jax
import jax.numpy as jnp
from jax import lax
from jax.experimental import pallas as pl
from jax.experimental.pallas import tpu as pltpu
from jax.sharding import PartitionSpec as P

BF16 = jnp.bfloat16
F32 = jnp.float32
NT = (((1,), (1,)), ((), ()))
TN = (((0,), (0,)), ((), ()))
VMEM = pl.BlockSpec(memory_space=pltpu.VMEM)
SMEM = pl.BlockSpec(memory_space=pltpu.SMEM)
PARAMS = pltpu.CompilerParams(vmem_limit_bytes=32 * 1024 * 1024)


def dot_nt(left, right):
    return lax.dot_general(left, right, NT, preferred_element_type=F32)


def edges_kernel(count_ref, rows_ref, cols_ref, order_ref, tiles_ref, m_ref, mt_ref, deg_ref, a_ref, p_ref):
    a_ref[...] = jnp.zeros_like(a_ref)
    tile = tiles_ref.shape[1]

    def add_slot(slot, carry):
        row = pl.multiple_of(rows_ref[slot] * tile, tile)
        col = pl.multiple_of(cols_ref[slot] * tile, tile)
        a_ref[pl.ds(row, tile), pl.ds(col, tile)] += tiles_ref[slot]
        return carry

    lax.fori_loop(0, count_ref[0], add_slot, 0)
    size = a_ref.shape[0]
    order = jnp.broadcast_to(order_ref[...], (size, size))
    places = lax.broadcasted_iota(jnp.int32, (size, size), 0)
    p_ref[...] = jnp.where(places == order, 1.0, 0.0).astype(BF16)
    step = 256
    for start in range(0, size, step):
        part = slice(start, start + step)
        m_ref[:, part] = dot_nt(a_ref[...], p_ref[part, :]).astype(BF16)
        mt_ref[:, part] = dot_nt(p_ref[...], a_ref[part, :]).astype(BF16)
    degree = dot_nt(jnp.ones((16, size), BF16), a_ref[...])
    high = jnp.floor(degree * (1.0 / 128.0))
    deg_ref[:, :size] = high.astype(BF16)
    deg_ref[:, size:] = (degree - 128.0 * high).astype(BF16)


def forward_kernel(m_ref, features_ref, deg_ref, send_ref):
    n_col, rows = send_ref.shape[0], send_ref.shape[1] - 16
    size = m_ref.shape[0]
    for start in range(0, n_col, 4):
        sums = jnp.dot(
            m_ref[start * rows : (start + 4) * rows, :], features_ref[...], preferred_element_type=F32
        ).astype(BF16)
        for k in range(4):
            send_ref[start + k, :rows, :] = sums[k * rows : (k + 1) * rows, :]
    for j in range(n_col):
        base = (j // 2) * 128
        send_ref[j, rows:, :128] = deg_ref[:, base : base + 128]
        send_ref[j, rows:, 128:] = deg_ref[:, size + base : size + base + 128]


def dense_kernel(half_ref, recv_ref, weight_ref, bias_ref, cot_ref, out_ref, send_ref):
    n_col, rows = recv_ref.shape[0], recv_ref.shape[1] - 16
    sums = recv_ref[0, :rows, :].astype(F32)
    deg_parts = recv_ref[0, rows:, :].astype(F32)
    for j in range(1, n_col):
        sums += recv_ref[j, :rows, :].astype(F32)
        deg_parts += recv_ref[j, rows:, :].astype(F32)
    deg_lanes = 128.0 * deg_parts[:1, :128] + deg_parts[:1, 128:]
    lane = lax.broadcasted_iota(jnp.int32, (rows, 128), 1)
    own = lax.broadcasted_iota(jnp.int32, (rows, 128), 0) + rows * half_ref[0]
    degree = jnp.sum(jnp.where(lane == own, deg_lanes, 0.0), axis=1, keepdims=True)
    scale = lax.rsqrt(jnp.maximum(degree, 1.0))
    agg = (sums * scale).astype(BF16)
    pre = jnp.dot(agg, weight_ref[...], preferred_element_type=F32) + bias_ref[...]
    sigma = jax.nn.sigmoid(pre)
    out_ref[...] = (pre * sigma).astype(BF16)
    grad = (cot_ref[...].astype(F32) * (sigma * (1.0 + pre * (1.0 - sigma)))).astype(BF16)
    dsum = (dot_nt(grad, weight_ref[...]) * scale).astype(BF16)
    weight_term = lax.dot_general(agg, grad, TN, preferred_element_type=F32).astype(BF16)
    bias_rows = split_rows(jnp.sum(grad.astype(F32), axis=0, keepdims=True))
    for j in range(n_col):
        send_ref[j, :rows, :] = dsum
        send_ref[j, rows : rows + 16, :] = weight_term[16 * j : 16 * (j + 1), :]
        send_ref[j, rows + 16 :, :] = bias_rows


def split_rows(row):
    high = row.astype(BF16)
    low = (row - high.astype(F32)).astype(BF16)
    index = lax.broadcasted_iota(jnp.int32, (16, row.shape[1]), 0)
    both = jnp.where(index == 0, high.astype(F32), jnp.where(index == 1, low.astype(F32), 0.0))
    return both.astype(BF16)


def backward_kernel(mt_ref, recv_ref, send_ref, grads_ref):
    n_col, rows = recv_ref.shape[0], recv_ref.shape[1] - 32
    n_row, own = send_ref.shape[0], send_ref.shape[1] - 32
    extra = recv_ref[0, rows:, :].astype(F32)
    for j in range(1, n_col):
        extra += recv_ref[j, rows:, :].astype(F32)
    weight_rows = extra[:16, :].astype(BF16)
    bias_rows = split_rows(jnp.sum(extra[16:, :], axis=0, keepdims=True))
    for j in range(n_col):
        grads_ref[j * rows : (j + 1) * rows, :] = recv_ref[j, :rows, :]
    group = 8
    for start in range(0, n_row, group):
        sums = jnp.dot(
            mt_ref[start * own : (start + group) * own, :], grads_ref[...], preferred_element_type=F32
        ).astype(BF16)
        for k in range(group):
            send_ref[start + k, :own, :] = sums[k * own : (k + 1) * own, :]
    for i in range(n_row):
        send_ref[i, own : own + 16, :] = weight_rows
        send_ref[i, own + 16 :, :] = bias_rows


def final_kernel(recv_ref, feature_ref, chunk_ref, bias_ref):
    n_row, own = recv_ref.shape[0], recv_ref.shape[1] - 32
    total = recv_ref[0].astype(F32)
    for i in range(1, n_row):
        total += recv_ref[i].astype(F32)
    feature_ref[...] = total[:own, :].astype(BF16)
    chunk_ref[...] = total[own : own + 16, :]
    bias_ref[...] = jnp.sum(total[own + 16 :, :], axis=0, keepdims=True)


def exchange(blocks, axis):
    return lax.all_to_all(blocks, axis, split_axis=0, concat_axis=0, tiled=True)


def spread(block, count, axis):
    return exchange(jnp.broadcast_to(block[None], (count,) + block.shape), axis)


def make_body(n_row, n_col):
    def body(
        features,
        node_order,
        tile_weights,
        tile_rows,
        tile_cols,
        tile_count,
        weight,
        bias_vector,
        cotangent,
    ):
        own, width = features.shape[1], features.shape[2]
        size = n_row * own
        rows = cotangent.shape[0]
        gathered = spread(features[0], n_row, "row").reshape(size, width)
        matrix, matrix_t, degree = pl.pallas_call(
            edges_kernel,
            out_shape=(
                jax.ShapeDtypeStruct((size, size), BF16),
                jax.ShapeDtypeStruct((size, size), BF16),
                jax.ShapeDtypeStruct((16, 2 * size), BF16),
            ),
            in_specs=[SMEM, SMEM, SMEM, VMEM, VMEM],
            out_specs=(VMEM, VMEM, VMEM),
            scratch_shapes=[pltpu.VMEM((size, size), BF16), pltpu.VMEM((size, size), BF16)],
            compiler_params=PARAMS,
            cost_estimate=pl.CostEstimate(flops=8 * size**3, bytes_accessed=5 * 2**20, transcendentals=0),
            name="edges",
        )(tile_count, tile_rows, tile_cols, node_order, tile_weights)
        send_sums = pl.pallas_call(
            forward_kernel,
            out_shape=jax.ShapeDtypeStruct((n_col, rows + 16, width), BF16),
            in_specs=[VMEM] * 3,
            out_specs=VMEM,
            compiler_params=PARAMS,
            name="forward",
        )(matrix, gathered, degree)
        recv_sums = exchange(send_sums, "col")
        half = (lax.axis_index("col") % 2).astype(jnp.int32).reshape(1)
        output, send_grads = pl.pallas_call(
            dense_kernel,
            out_shape=(
                jax.ShapeDtypeStruct((rows, width), BF16),
                jax.ShapeDtypeStruct((n_col, rows + 32, width), BF16),
            ),
            in_specs=[SMEM] + [VMEM] * 4,
            out_specs=(VMEM, VMEM),
            compiler_params=PARAMS,
            name="dense",
        )(half, recv_sums, weight, bias_vector.reshape(1, width), cotangent)
        recv_grads = exchange(send_grads, "col")
        send_back = pl.pallas_call(
            backward_kernel,
            out_shape=jax.ShapeDtypeStruct((n_row, own + 32, width), BF16),
            in_specs=[VMEM] * 2,
            out_specs=VMEM,
            scratch_shapes=[pltpu.VMEM((size, width), BF16)],
            compiler_params=PARAMS,
            name="backward",
        )(matrix_t, recv_grads)
        recv_back = exchange(send_back, "row")
        feature_grad, chunk, bias_grad = pl.pallas_call(
            final_kernel,
            out_shape=(
                jax.ShapeDtypeStruct((own, width), BF16),
                jax.ShapeDtypeStruct((16, width), F32),
                jax.ShapeDtypeStruct((1, width), F32),
            ),
            in_specs=[VMEM],
            out_specs=(VMEM,) * 3,
            compiler_params=PARAMS,
            name="final",
        )(recv_back)
        weight_grad = spread(chunk, n_col, "col").reshape(width, width)
        return (output, feature_grad[None], weight_grad, bias_grad.reshape(width))

    return body


def solution(mesh):
    return jax.shard_map(
        make_body(mesh.shape["row"], mesh.shape["col"]),
        mesh=mesh,
        in_specs=(
            P("col", "row", None),
            P("col", None),
            P(("row", "col"), None, None),
            P(("row", "col")),
            P(("row", "col")),
            P(("row", "col")),
            P(),
            P(),
            P(("row", "col"), None),
        ),
        out_specs=(P(("row", "col"), None), P("col", "row", None), P(), P()),
        check_vma=False,
    )
```

time: 1310 us -> 163 us (0.12)
  the two profiles are of different devices: /device:TPU:1 before, /device:TPU:32 now
where the time goes in v1:
time: 163 us
  blocking collectives  87.1 us (53%)
  waiting for transfers between devices  35 us (21%)
  starting transfers between devices  22.6 us (14%)
  Pallas kernels  9.63 us (6%)
  local copies, waits for them, and re-layouts  6.86 us (4%)
    all_to_all x3, blocking collectives, exchange(): return lax.all_to_all(blocks, axis, split_axis=0, concat_axis=0, tiled=True)  87.1 us
    all_to_all x2, waiting for transfers between devices, exchange(): return lax.all_to_all(blocks, axis, split_axis=0, concat_axis=0, tiled=True)  35 us
    all_to_all x2, starting transfers between devices, exchange(): return lax.all_to_all(blocks, axis, split_axis=0, concat_axis=0, tiled=True)  22.6 us
    pallas_call x1, Pallas kernels, body(): pl.pallas_call(edges_kernel, out_shape=(jax.ShapeDtypeStruct((size, size)...  5.82 us
    unnamed x19, local copies, waits for them, and re-layouts  5.26 us
  transfers between devices with their start and end apart: 2, of which 2 were waited for; matrix products, arithmetic and copies ran while one was open for 0% of the time, Pallas kernels for 4%

profile of v1, /device:TPU:32, one launch (start us, length us, event | category | flops | bytes accessed | tf_op | source)
XLA Modules:
  0.0 162.5 jit_solution(16693511723190987324)
XLA Ops:
  0.6 1.6 broadcast_in_dim.17
  2.2 18.0 %all-to-all-start = ((bf16[32,32,256]{2,1,0:T(8,128)(2,1)}), bf16[32,32,256]{2,1,0:T(8,128)(2,1)S(1)}, u32[]{:S(2)}, u32[]{:S(2)}) async-start(bf16[32,32,256]{2,1,0:T(8,128)(2,1)} %broadcast_in_dim.17), calls=%async_computation | async-start | bytes 1048576 | tf_op jit(solution)/shard_map/all_to_all | solution.py:129
  20.8 0.0 copy-start.5
  20.9 1.2 copy-done.5
  22.1 0.0 copy-start.6
  22.1 0.7 copy-done.6
  22.8 0.0 copy-start.7
  22.8 0.7 copy-done.7
  23.4 0.0 copy-start.8
  23.4 0.7 copy-done.8
  24.1 5.8 %edges.1 = (bf16[1024,1024]{1,0:T(8,128)(2,1)S(1)}, bf16[1024,1024]{1,0:T(8,128)(2,1)S(1)}, bf16[16,2048]{1,0:T(8,128)(2,1)S(1)}) custom-call(s32[1]{0:T(128)S(6)} %copy.14.count_ref, s32[32]{0:T(128)S(1)} %copy-done.7, s32[32]{0:T(128)S(1)} %copy-done.8, s32[1,1024]{1,0:T(1,128)S(1)} %copy-done.6, bf16[32,128,128]{2,1,0:T(8,128)(2,1)S(1)} %copy-done.5), custom_call_target="tpu_custom_call" | custom-call | flops 8589934592 | bytes 5242880 | tf_op jit(solution)/shard_map/edges/pallas_call | solution.py:152
  29.9 0.0 copy-start
  29.9 1.3 copy-done
  31.2 22.7 %all-to-all-done = bf16[32,32,256]{2,1,0:T(8,128)(2,1)S(1)} async-done(((bf16[32,32,256]{2,1,0:T(8,128)(2,1)}), bf16[32,32,256]{2,1,0:T(8,128)(2,1)S(1)}, u32[]{:S(2)}, u32[]{:S(2)}) %all-to-all-start) | async-done | bytes 524320 | tf_op jit(solution)/shard_map/all_to_all | solution.py:129
  53.9 0.0 copy-start.2
  53.9 0.0 copy-start.3
  54.0 0.0 copy-start.4
  54.0 1.5 forward.1
  55.5 0.0 copy-start.1
  55.5 4.6 %all-to-all-start.1 = ((bf16[16,80,256]{2,1,0:T(8,128)(2,1)}), bf16[16,80,256]{2,1,0:T(8,128)(2,1)S(1)}, u32[]{:S(2)}, u32[]{:S(2)}) async-start(bf16[16,80,256]{2,1,0:T(8,128)(2,1)} %forward.1), calls=%async_computation.1 | async-start | bytes 1310720 | tf_op jit(solution)/shard_map/all_to_all | solution.py:129
  60.2 12.3 %all-to-all-done.1.recv_ref = bf16[16,80,256]{2,1,0:T(8,128)(2,1)S(1)} async-done(((bf16[16,80,256]{2,1,0:T(8,128)(2,1)}), bf16[16,80,256]{2,1,0:T(8,128)(2,1)S(1)}, u32[]{:S(2)}, u32[]{:S(2)}) %all-to-all-start.1) | async-done | bytes 655392 | tf_op jit(solution)/shard_map/all_to_all | solution.py:129
  72.4 0.0 copy-done.2
  72.4 0.0 copy-done.3
  72.4 0.0 copy-done.4
  72.4 0.9 dense.1
  73.3 16.1 %all_to_all.25.recv_ref = bf16[16,96,256]{2,1,0:T(8,128)(2,1)S(1)} all-to-all(bf16[16,96,256]{2,1,0:T(8,128)(2,1)S(1)} %get-tuple-element.16), channel_id=1, replica_groups=mesh['row'=32,'col'=16] {'col'}, dimensions={0} | all-to-all | bytes 1572864 | tf_op jit(solution)/shard_map/all_to_all | solution.py:129
  89.4 0.0 copy-done.1
  89.4 0.7 backward.1
  90.1 60.5 %all_to_all.26.recv_ref = bf16[32,64,256]{2,1,0:T(8,128)(2,1)S(1)} all-to-all(bf16[32,64,256]{2,1,0:T(8,128)(2,1)S(1)} %backward.1), channel_id=1, replica_groups=mesh['row'=32,'col'=16] {'row'}, dimensions={0} | all-to-all | bytes 2097152 | tf_op jit(solution)/shard_map/all_to_all | solution.py:129
  150.7 0.7 final.1
  151.4 10.5 %all_to_all.27 = f32[16,16,256]{2,1,0:T(8,128)S(1)} all-to-all(f32[16,16,256]{2,1,0:T(8,128)S(1)} %broadcast_in_dim.19), channel_id=1, replica_groups=mesh['row'=32,'col'=16] {'col'}, dimensions={0} | all-to-all | bytes 524288 | tf_op jit(solution)/shard_map/all_to_all | solution.py:129
  161.8 0.7 copy.15
  (1 shorter events, 0.0 us)
Async XLA Ops:
  2.2 51.7 %all-to-all-start = ((bf16[32,32,256]{2,1,0:T(8,128)(2,1)}), bf16[32,32,256]{2,1,0:T(8,128)(2,1)S(1)}, u32[]{:S(2)}, u32[]{:S(2)}) async-start(bf16[32,32,256]{2,1,0:T(8,128)(2,1)} %broadcast_in_dim.17), calls=%async_computation | async-start | bytes 1048576 | tf_op jit(solution)/shard_map/all_to_all | solution.py:129
  20.8 1.2 copy-start.5
  22.1 0.7 copy-start.6
  22.8 0.7 copy-start.7
  23.4 0.7 copy-start.8
  29.9 1.3 copy-start
  53.9 18.5 %copy-start.2 = (bf16[256,256]{1,0:T(8,128)(2,1)S(1)}, bf16[256,256]{1,0:T(8,128)(2,1)}, u32[]{:S(2)}) copy-start(bf16[256,256]{1,0:T(8,128)(2,1)} %weight_ref.1) | copy-start | bytes 393220
  53.9 18.5 %copy-start.3 = (bf16[64,256]{1,0:T(8,128)(2,1)S(1)}, bf16[64,256]{1,0:T(8,128)(2,1)}, u32[]{:S(2)}) copy-start(bf16[64,256]{1,0:T(8,128)(2,1)} %cot_ref.1) | copy-start | bytes 98308
  54.0 18.5 %copy-start.4 = (f32[256]{0:T(256)S(1)}, f32[256]{0:T(256)}, u32[]{:S(2)}) copy-start(f32[256]{0:T(256)} %param.16) | copy-start | bytes 3076
  55.5 33.9 %copy-start.1 = (bf16[1024,1024]{1,0:T(8,128)(2,1)S(1)}, bf16[1024,1024]{1,0:T(8,128)(2,1)}, u32[]{:S(2)}) copy-start(bf16[1024,1024]{1,0:T(8,128)(2,1)} %copy-done) | copy-start | bytes 6291460
  55.5 16.9 %all-to-all-start.1 = ((bf16[16,80,256]{2,1,0:T(8,128)(2,1)}), bf16[16,80,256]{2,1,0:T(8,128)(2,1)S(1)}, u32[]{:S(2)}, u32[]{:S(2)}) async-start(bf16[16,80,256]{2,1,0:T(8,128)(2,1)} %forward.1), calls=%async_computation.1 | async-start | bytes 1310720 | tf_op jit(solution)/shard_map/all_to_all | solution.py:129

commit v2 on v1

v2 whole, which is shorter than its diff:
```python
import jax
import jax.numpy as jnp
from jax import lax
from jax.experimental import pallas as pl
from jax.experimental.pallas import tpu as pltpu
from jax.sharding import Mesh, PartitionSpec as P

BF16 = jnp.bfloat16
F32 = jnp.float32
LANES = 128
HALVES = 2
NT = (((1,), (1,)), ((), ()))
TN = (((0,), (0,)), ((), ()))
VMEM = pl.BlockSpec(memory_space=pltpu.VMEM)
SMEM = pl.BlockSpec(memory_space=pltpu.SMEM)
PARAMS = pltpu.CompilerParams(vmem_limit_bytes=32 * 1024 * 1024)


def dot_nt(left, right):
    return lax.dot_general(left, right, NT, preferred_element_type=F32)


def rows_block(rows, height=8):
    index = lax.broadcasted_iota(jnp.int32, (height, LANES), 0)
    block = jnp.zeros((height, LANES), F32)
    for k, row in enumerate(rows):
        block = jnp.where(index == k, row, block)
    return block


def bias_block(row):
    high = row.astype(BF16).astype(F32)
    low = row - high
    return rows_block([high[:, :LANES], high[:, LANES:], low[:, :LANES], low[:, LANES:]]).astype(BF16)


def spread_kernel(block_ref, out_ref):
    for i in range(out_ref.shape[0]):
        out_ref[i] = block_ref[0]


def edges_kernel(count_ref, rows_ref, cols_ref, order_ref, tiles_ref, m_ref, mt_ref, deg_ref, a_ref, p_ref):
    a_ref[...] = jnp.zeros_like(a_ref)
    tile = tiles_ref.shape[1]

    def add_slot(slot, carry):
        row = pl.multiple_of(rows_ref[slot] * tile, tile)
        col = pl.multiple_of(cols_ref[slot] * tile, tile)
        a_ref[pl.ds(row, tile), pl.ds(col, tile)] += tiles_ref[slot]
        return carry

    lax.fori_loop(0, count_ref[0], add_slot, 0)
    size = a_ref.shape[0]
    order = jnp.broadcast_to(order_ref[...], (size, size))
    places = lax.broadcasted_iota(jnp.int32, (size, size), 0)
    p_ref[...] = jnp.where(places == order, 1.0, 0.0).astype(BF16)
    step = 256
    for start in range(0, size, step):
        part = slice(start, start + step)
        m_ref[:, part] = dot_nt(a_ref[...], p_ref[part, :]).astype(BF16)
        mt_ref[:, part] = dot_nt(p_ref[...], a_ref[part, :]).astype(BF16)
    degree = dot_nt(jnp.ones((16, size), BF16), a_ref[...])[:8, :]
    high = jnp.floor(degree * (1.0 / 128.0))
    index = lax.broadcasted_iota(jnp.int32, degree.shape, 0)
    deg_ref[...] = jnp.where(index == 0, high, degree - 128.0 * high).astype(BF16)


def forward_kernel(m_ref, features_ref, deg_ref, send_ref):
    n_col = send_ref.shape[0]
    rows = m_ref.shape[0] // n_col
    group = 4
    for start in range(0, n_col, group):
        sums = jnp.dot(
            m_ref[start * rows : (start + group) * rows, :], features_ref[...], preferred_element_type=F32
        ).astype(BF16)
        for k in range(group):
            send_ref[start + k, :rows, :] = sums[k * rows : (k + 1) * rows, :LANES]
            send_ref[start + k, rows : 2 * rows, :] = sums[k * rows : (k + 1) * rows, LANES:]
    for j in range(n_col):
        base = j * rows // LANES * LANES
        send_ref[j, 2 * rows :, :] = deg_ref[:, base : base + LANES]


def dense_kernel(half_ref, recv_ref, weight_ref, bias_ref, cot_ref, out_ref, send_ref):
    n_col, rows = recv_ref.shape[0], cot_ref.shape[0]
    total = recv_ref[0].astype(F32)
    for j in range(1, n_col):
        total += recv_ref[j].astype(F32)
    sums = jnp.concatenate([total[:rows, :], total[rows : 2 * rows, :]], axis=1)
    deg_lanes = 128.0 * total[2 * rows : 2 * rows + 1, :] + total[2 * rows + 1 : 2 * rows + 2, :]
    lane = lax.broadcasted_iota(jnp.int32, (rows, LANES), 1)
    own = lax.broadcasted_iota(jnp.int32, (rows, LANES), 0) + rows * half_ref[0]
    degree = jnp.sum(jnp.where(lane == own, deg_lanes, 0.0), axis=1, keepdims=True)
    scale = lax.rsqrt(jnp.maximum(degree, 1.0))
    agg = (sums * scale).astype(BF16)
    pre = jnp.dot(agg, weight_ref[...], preferred_element_type=F32) + bias_ref[...]
    sigma = jax.nn.sigmoid(pre)
    out_ref[...] = (pre * sigma).astype(BF16)
    grad = (cot_ref[...].astype(F32) * (sigma * (1.0 + pre * (1.0 - sigma)))).astype(BF16)
    dsum = (dot_nt(grad, weight_ref[...]) * scale).astype(BF16)
    weight_term = lax.dot_general(agg, grad, TN, preferred_element_type=F32)
    bias_rows = bias_block(jnp.sum(grad.astype(F32), axis=0, keepdims=True))
    part = weight_term.shape[0] // (HALVES * n_col)
    for j in range(n_col):
        chunk = jnp.concatenate(
            [weight_term[(h * n_col + j) * part : (h * n_col + j + 1) * part, :] for h in range(HALVES)], axis=0
        ).astype(BF16)
        send_ref[j, :rows, :] = dsum[:, :LANES]
        send_ref[j, rows : 2 * rows, :] = dsum[:, LANES:]
        send_ref[j, 2 * rows : 2 * rows + 16, :] = chunk[:, :LANES]
        send_ref[j, 2 * rows + 16 : 2 * rows + 32, :] = chunk[:, LANES:]
        send_ref[j, 2 * rows + 32 :, :] = bias_rows


def backward_kernel(mt_ref, recv_ref, send_ref, grads_ref):
    n_col, n_row = recv_ref.shape[0], send_ref.shape[0]
    size = mt_ref.shape[0]
    rows, own = size // n_col, size // n_row
    extra = recv_ref[0, 2 * rows :, :].astype(F32)
    for j in range(1, n_col):
        extra += recv_ref[j, 2 * rows :, :].astype(F32)
    bias = extra[32:34, :] + extra[34:36, :]
    bias_rows = bias_block(jnp.concatenate([bias[:1, :], bias[1:, :]], axis=1))
    for j in range(n_col):
        grads_ref[j * rows : (j + 1) * rows, :LANES] = recv_ref[j, :rows, :]
        grads_ref[j * rows : (j + 1) * rows, LANES:] = recv_ref[j, rows : 2 * rows, :]
    group = 8
    for start in range(0, n_row, group):
        sums = jnp.dot(
            mt_ref[start * own : (start + group) * own, :], grads_ref[...], preferred_element_type=F32
        ).astype(BF16)
        for k in range(group):
            send_ref[start + k, :own, :] = sums[k * own : (k + 1) * own, :LANES]
            send_ref[start + k, own : 2 * own, :] = sums[k * own : (k + 1) * own, LANES:]
    for h in range(HALVES):
        chunk = jnp.concatenate([extra[8 * h : 8 * h + 8, :], extra[16 + 8 * h : 24 + 8 * h, :]], axis=0).astype(BF16)
        for z in range(n_row // HALVES):
            send_ref[h * (n_row // HALVES) + z, 2 * own : 2 * own + 16, :] = chunk
    for i in range(n_row):
        send_ref[i, 2 * own + 16 :, :] = bias_rows


def final_kernel(recv_ref, feature_ref, bias_ref, spread_ref):
    n_row, own = recv_ref.shape[0], feature_ref.shape[0]
    total = recv_ref[0].astype(F32)
    for i in range(1, n_row):
        total += recv_ref[i].astype(F32)
    feature_ref[:, :LANES] = total[:own, :].astype(BF16)
    feature_ref[:, LANES:] = total[own : 2 * own, :].astype(BF16)
    base = 2 * own
    chunk = jnp.concatenate([total[base : base + 8, :], total[base + 8 : base + 16, :]], axis=1)
    for i in range(spread_ref.shape[0]):
        spread_ref[i] = chunk
    bias = total[base + 16 : base + 18, :] + total[base + 18 : base + 20, :]
    bias_ref[:, :LANES] = bias[:1, :]
    bias_ref[:, LANES:] = bias[1:, :]


def exchange(blocks, axes):
    return lax.all_to_all(blocks, axes, split_axis=0, concat_axis=0, tiled=True)


def call(kernel, out_shape, in_specs, scratch=(), **options):
    several = isinstance(out_shape, tuple)
    return pl.pallas_call(
        kernel,
        out_shape=out_shape,
        in_specs=in_specs,
        out_specs=(VMEM,) * len(out_shape) if several else VMEM,
        scratch_shapes=list(scratch),
        compiler_params=PARAMS,
        name=kernel.__name__,
        **options,
    )


def make_body(n_row, n_col):
    row_axes = ("half", "rest")

    def body(
        features,
        node_order,
        tile_weights,
        tile_rows,
        tile_cols,
        tile_count,
        weight,
        bias_vector,
        cotangent,
    ):
        own, width = features.shape[1], features.shape[2]
        size = n_row * own
        rows = cotangent.shape[0]
        shape = jax.ShapeDtypeStruct
        sends = call(spread_kernel, shape((n_row, own, width), BF16), [VMEM])(features)
        gathered = exchange(sends, row_axes).reshape(size, width)
        matrix, matrix_t, degree = call(
            edges_kernel,
            (shape((size, size), BF16), shape((size, size), BF16), shape((8, size), BF16)),
            [SMEM, SMEM, SMEM, VMEM, VMEM],
            [pltpu.VMEM((size, size), BF16), pltpu.VMEM((size, size), BF16)],
            cost_estimate=pl.CostEstimate(flops=8 * size**3, bytes_accessed=5 * 2**20, transcendentals=0),
        )(tile_count, tile_rows, tile_cols, node_order, tile_weights)
        send_sums = call(forward_kernel, shape((n_col, 2 * rows + 8, LANES), BF16), [VMEM] * 3)(
            matrix, gathered, degree
        )
        recv_sums = exchange(send_sums, "col")
        half = (lax.axis_index("col") * rows % LANES // rows).astype(jnp.int32).reshape(1)
        output, send_grads = call(
            dense_kernel,
            (shape((rows, width), BF16), shape((n_col, 2 * rows + 40, LANES), BF16)),
            [SMEM] + [VMEM] * 4,
        )(half, recv_sums, weight, bias_vector.reshape(1, width), cotangent)
        recv_grads = exchange(send_grads, "col")
        send_back = call(
            backward_kernel,
            shape((n_row, 2 * own + 24, LANES), BF16),
            [VMEM] * 2,
            [pltpu.VMEM((size, width), BF16)],
        )(matrix_t, recv_grads)
        recv_back = exchange(send_back, row_axes)
        feature_grad, bias_grad, send_weight = call(
            final_kernel,
            (
                shape((own, width), BF16),
                shape((1, width), F32),
                shape((HALVES * n_col, 8, width), F32),
            ),
            [VMEM],
        )(recv_back)
        weight_grad = exchange(send_weight, ("half", "col")).reshape(width, width)
        return (output, feature_grad[None], weight_grad, bias_grad.reshape(width))

    return body


def solution(mesh):
    n_row, n_col = mesh.shape["row"], mesh.shape["col"]
    row = ("half", "rest")
    split = Mesh(mesh.devices.reshape(HALVES, n_row // HALVES, n_col), row + ("col",))
    return jax.shard_map(
        make_body(n_row, n_col),
        mesh=split,
        in_specs=(
            P("col", row, None),
            P("col", None),
            P(row + ("col",), None, None),
            P(row + ("col",)),
            P(row + ("col",)),
            P(row + ("col",)),
            P(),
            P(),
            P(row + ("col",), None),
        ),
        out_specs=(P(row + ("col",), None), P("col", row, None), P(), P()),
        check_vma=False,
    )
```

time: 163 us -> 149 us (0.914)
  the two profiles are of different devices: /device:TPU:32 before, /device:TPU:1 now
where the time goes in v2:
time: 149 us; the launch traced here: 147 us
  blocking collectives  73.2 us (49%)
  waiting for transfers between devices  31 us (21%)
  starting transfers between devices  24.7 us (17%)
  Pallas kernels  10.9 us (7%)
  local copies, waits for them, and re-layouts  5.98 us (4%)
    all_to_all x3, blocking collectives, exchange(): return lax.all_to_all(blocks, axes, split_axis=0, concat_axis=0, tiled=True)  73.2 us
    all_to_all x2, waiting for transfers between devices, exchange(): return lax.all_to_all(blocks, axes, split_axis=0, concat_axis=0, tiled=True)  31 us
    all_to_all x2, starting transfers between devices, exchange(): return lax.all_to_all(blocks, axes, split_axis=0, concat_axis=0, tiled=True)  24.7 us
    pallas_call x1, Pallas kernels, body(): call(edges_kernel, (shape((size, size), BF16), shape((size, size), BF16),...  6.2 us
    unnamed x21, local copies, waits for them, and re-layouts  5.98 us
  transfers between devices with their start and end apart: 2, of which 2 were waited for; matrix products, arithmetic and copies ran while one was open for 0% of the time, Pallas kernels for 4%

profile of v2, /device:TPU:1, one launch (start us, length us, event | category | flops | bytes accessed | tf_op | source)
XLA Modules:
  0.0 147.1 jit_solution(11427615563901223691)
XLA Ops:
  0.6 0.0 copy-start.4
  0.6 0.7 copy-done.4
  1.3 0.9 spread_kernel.1
  2.2 18.7 %all-to-all-start = ((bf16[32,32,256]{2,1,0:T(8,128)(2,1)}), bf16[32,32,256]{2,1,0:T(8,128)(2,1)S(1)}, u32[]{:S(2)}, u32[]{:S(2)}) async-start(bf16[32,32,256]{2,1,0:T(8,128)(2,1)} %spread_kernel.1), calls=%async_computation | async-start | bytes 1048576 | tf_op jit(solution)/shard_map/all_to_all | solution.py:160
  21.5 0.0 copy-start.6
  21.5 1.2 copy-done.6
  22.8 0.0 copy-start.7
  22.8 0.7 copy-done.7
  23.4 0.0 copy-start.8
  23.4 0.7 copy-done.8
  24.1 0.0 copy-start.9
  24.1 0.7 copy-done.9
  24.8 6.2 %edges_kernel.1 = (bf16[1024,1024]{1,0:T(8,128)(2,1)S(1)}, bf16[1024,1024]{1,0:T(8,128)(2,1)S(1)}, bf16[8,1024]{1,0:T(8,128)(2,1)S(1)}) custom-call(s32[1]{0:T(128)S(6)} %copy.14.count_ref, s32[32]{0:T(128)S(1)} %copy-done.8, s32[32]{0:T(128)S(1)} %copy-done.9, s32[1,1024]{1,0:T(1,128)S(1)} %copy-done.7, bf16[32,128,128]{2,1,0:T(8,128)(2,1)S(1)} %copy-done.6), custom_call_target="tpu_custom_call" | custom-call | flops 8589934592 | bytes 5242880 | tf_op jit(solution)/shard_map/edges_kernel/pallas_call | solution.py:197
  31.0 0.0 copy-start
  31.0 1.3 copy-done
  32.3 20.7 %all-to-all-done = bf16[32,32,256]{2,1,0:T(8,128)(2,1)S(1)} async-done(((bf16[32,32,256]{2,1,0:T(8,128)(2,1)}), bf16[32,32,256]{2,1,0:T(8,128)(2,1)S(1)}, u32[]{:S(2)}, u32[]{:S(2)}) %all-to-all-start) | async-done | bytes 524320 | tf_op jit(solution)/shard_map/all_to_all | solution.py:160
  53.0 0.0 copy-start.2
  53.0 0.0 copy-start.3
  53.1 0.0 copy-start.5
  53.1 1.5 %forward_kernel.1 = bf16[16,136,128]{2,1,0:T(8,128)(2,1)} custom-call(bf16[1024,1024]{1,0:T(8,128)(2,1)S(1)} %get-tuple-element.12.m_ref, bf16[1024,256]{1,0:T(8,128)(2,1)S(1)} %bitcast.6, bf16[8,1024]{1,0:T(8,128)(2,1)S(1)} %get-tuple-element.13.deg_ref), custom_call_target="tpu_custom_call" | custom-call | tf_op jit(solution)/shard_map/forward_kernel/pallas_call | solution.py:204
  54.6 0.0 copy-start.1
  54.6 6.1 %all-to-all-start.1 = ((bf16[16,136,128]{2,1,0:T(8,128)(2,1)}), bf16[16,136,128]{2,1,0:T(8,128)(2,1)S(1)}, u32[]{:S(2)}, u32[]{:S(2)}) async-start(bf16[16,136,128]{2,1,0:T(8,128)(2,1)} %forward_kernel.1), calls=%async_computation.1 | async-start | bytes 1114112 | tf_op jit(solution)/shard_map/all_to_all | solution.py:160
  60.7 10.2 %all-to-all-done.1.recv_ref = bf16[16,136,128]{2,1,0:T(8,128)(2,1)S(1)} async-done(((bf16[16,136,128]{2,1,0:T(8,128)(2,1)}), bf16[16,136,128]{2,1,0:T(8,128)(2,1)S(1)}, u32[]{:S(2)}, u32[]{:S(2)}) %all-to-all-start.1) | async-done | bytes 557088 | tf_op jit(solution)/shard_map/all_to_all | solution.py:160
  70.9 0.0 copy-done.2
  70.9 0.0 copy-done.3
  70.9 0.0 copy-done.5
  70.9 0.9 dense_kernel.1
  71.8 15.5 %all_to_all.25.recv_ref = bf16[16,168,128]{2,1,0:T(8,128)(2,1)S(1)} all-to-all(bf16[16,168,128]{2,1,0:T(8,128)(2,1)S(1)} %get-tuple-element.16), channel_id=1, replica_groups=mesh['half'=2,'rest'=16,'col'=16] {'col'}, dimensions={0} | all-to-all | bytes 1376256 | tf_op jit(solution)/shard_map/all_to_all | solution.py:160
  87.3 0.0 copy-done.1
  87.3 0.7 backward_kernel.1
  88.0 44.6 %all_to_all.26.recv_ref = bf16[32,88,128]{2,1,0:T(8,128)(2,1)S(1)} all-to-all(bf16[32,88,128]{2,1,0:T(8,128)(2,1)S(1)} %backward_kernel.1), channel_id=1, replica_groups=mesh['half'=2,'rest'=16,'col'=16] {'half','rest'}, dimensions={0} | all-to-all | bytes 1441792 | tf_op jit(solution)/shard_map/all_to_all | solution.py:160
  132.6 0.7 final_kernel.1
  133.3 13.1 %all_to_all.27 = f32[32,8,256]{2,1,0:T(8,128)S(1)} all-to-all(f32[32,8,256]{2,1,0:T(8,128)S(1)} %get-tuple-element.18), channel_id=1, replica_groups=mesh['half'=2,'rest'=16,'col'=16] {'half','col'}, dimensions={0} | all-to-all | bytes 524288 | tf_op jit(solution)/shard_map/all_to_all | solution.py:160
  146.4 0.7 copy.15
Async XLA Ops:
  0.6 0.7 copy-start.4
  2.2 50.8 %all-to-all-start = ((bf16[32,32,256]{2,1,0:T(8,128)(2,1)}), bf16[32,32,256]{2,1,0:T(8,128)(2,1)S(1)}, u32[]{:S(2)}, u32[]{:S(2)}) async-start(bf16[32,32,256]{2,1,0:T(8,128)(2,1)} %spread_kernel.1), calls=%async_computation | async-start | bytes 1048576 | tf_op jit(solution)/shard_map/all_to_all | solution.py:160
  21.5 1.2 copy-start.6
  22.8 0.7 copy-start.7
  23.4 0.7 copy-start.8
  24.1 0.7 copy-start.9
  31.0 1.3 copy-start
  53.0 17.8 %copy-start.2 = (bf16[256,256]{1,0:T(8,128)(2,1)S(1)}, bf16[256,256]{1,0:T(8,128)(2,1)}, u32[]{:S(2)}) copy-start(bf16[256,256]{1,0:T(8,128)(2,1)} %weight_ref.1) | copy-start | bytes 393220
  53.0 17.8 %copy-start.3 = (bf16[64,256]{1,0:T(8,128)(2,1)S(1)}, bf16[64,256]{1,0:T(8,128)(2,1)}, u32[]{:S(2)}) copy-start(bf16[64,256]{1,0:T(8,128)(2,1)} %cot_ref.1) | copy-start | bytes 98308
  53.1 17.8 %copy-start.5 = (f32[256]{0:T(256)S(1)}, f32[256]{0:T(256)}, u32[]{:S(2)}) copy-start(f32[256]{0:T(256)} %param.16) | copy-start | bytes 3076
  54.6 32.7 %copy-start.1 = (bf16[1024,1024]{1,0:T(8,128)(2,1)S(1)}, bf16[1024,1024]{1,0:T(8,128)(2,1)}, u32[]{:S(2)}) copy-start(bf16[1024,1024]{1,0:T(8,128)(2,1)} %copy-done) | copy-start | bytes 6291460
  54.6 16.3 %all-to-all-start.1 = ((bf16[16,136,128]{2,1,0:T(8,128)(2,1)}), bf16[16,136,128]{2,1,0:T(8,128)(2,1)S(1)}, u32[]{:S(2)}, u32[]{:S(2)}) async-start(bf16[16,136,128]{2,1,0:T(8,128)(2,1)} %forward_kernel.1), calls=%async_computation.1 | async-start | bytes 1114112 | tf_op jit(solution)/shard_map/all_to_all | solution.py:160

commit v3 on v2

--- a/solution.py
+++ b/solution.py
@@ -8,7 +8,7 @@
 BF16 = jnp.bfloat16
 F32 = jnp.float32
 LANES = 128
-HALVES = 2
+HALVES, FAR, NEAR = 2, 8, 2
 NT = (((1,), (1,)), ((), ()))
 TN = (((0,), (0,)), ((), ()))
 VMEM = pl.BlockSpec(memory_space=pltpu.VMEM)
@@ -36,7 +36,14 @@
 
 def spread_kernel(block_ref, out_ref):
     for i in range(out_ref.shape[0]):
-        out_ref[i] = block_ref[0]
+        out_ref[i] = block_ref[...].reshape(out_ref.shape[1:])
+
+
+def exchanged_place(place, own):
+    low, block = place & (own - 1), place >> (own.bit_length() - 1)
+    near, block = block & (NEAR - 1), block >> (NEAR.bit_length() - 1)
+    far, half = block & (FAR - 1), block >> (FAR.bit_length() - 1)
+    return ((half * NEAR + near) * FAR + far) * own + low
 
 
 def edges_kernel(count_ref, rows_ref, cols_ref, order_ref, tiles_ref, m_ref, mt_ref, deg_ref, a_ref, p_ref):
@@ -51,7 +58,8 @@
 
     lax.fori_loop(0, count_ref[0], add_slot, 0)
     size = a_ref.shape[0]
-    order = jnp.broadcast_to(order_ref[...], (size, size))
+    own = size // (HALVES * FAR * NEAR)
+    order = jnp.broadcast_to(exchanged_place(order_ref[...], own), (size, size))
     places = lax.broadcasted_iota(jnp.int32, (size, size), 0)
     p_ref[...] = jnp.where(places == order, 1.0, 0.0).astype(BF16)
     step = 256
@@ -100,11 +108,9 @@
     dsum = (dot_nt(grad, weight_ref[...]) * scale).astype(BF16)
     weight_term = lax.dot_general(agg, grad, TN, preferred_element_type=F32)
     bias_rows = bias_block(jnp.sum(grad.astype(F32), axis=0, keepdims=True))
-    part = weight_term.shape[0] // (HALVES * n_col)
+    weight_term = weight_term.astype(BF16)
     for j in range(n_col):
-        chunk = jnp.concatenate(
-            [weight_term[(h * n_col + j) * part : (h * n_col + j + 1) * part, :] for h in range(HALVES)], axis=0
-        ).astype(BF16)
+        chunk = weight_term[16 * j : 16 * (j + 1), :]
         send_ref[j, :rows, :] = dsum[:, :LANES]
         send_ref[j, rows : 2 * rows, :] = dsum[:, LANES:]
         send_ref[j, 2 * rows : 2 * rows + 16, :] = chunk[:, :LANES]
@@ -113,45 +119,60 @@
 
 
 def backward_kernel(mt_ref, recv_ref, send_ref, grads_ref):
-    n_col, n_row = recv_ref.shape[0], send_ref.shape[0]
+    n_col, n_near = recv_ref.shape[0], send_ref.shape[0]
     size = mt_ref.shape[0]
-    rows, own = size // n_col, size // n_row
+    rows, own = size // n_col, size // (n_near * FAR)
     extra = recv_ref[0, 2 * rows :, :].astype(F32)
     for j in range(1, n_col):
         extra += recv_ref[j, 2 * rows :, :].astype(F32)
-    bias = extra[32:34, :] + extra[34:36, :]
-    bias_rows = bias_block(jnp.concatenate([bias[:1, :], bias[1:, :]], axis=1))
+    chunk = extra[:32, :].astype(BF16)
+    bias_rows = merged_bias(extra[32:, :])
     for j in range(n_col):
         grads_ref[j * rows : (j + 1) * rows, :LANES] = recv_ref[j, :rows, :]
         grads_ref[j * rows : (j + 1) * rows, LANES:] = recv_ref[j, rows : 2 * rows, :]
-    group = 8
-    for start in range(0, n_row, group):
+    for i in range(n_near):
         sums = jnp.dot(
-            mt_ref[start * own : (start + group) * own, :], grads_ref[...], preferred_element_type=F32
+            mt_ref[i * FAR * own : (i + 1) * FAR * own, :], grads_ref[...], preferred_element_type=F32
         ).astype(BF16)
-        for k in range(group):
-            send_ref[start + k, :own, :] = sums[k * own : (k + 1) * own, :LANES]
-            send_ref[start + k, own : 2 * own, :] = sums[k * own : (k + 1) * own, LANES:]
-    for h in range(HALVES):
-        chunk = jnp.concatenate([extra[8 * h : 8 * h + 8, :], extra[16 + 8 * h : 24 + 8 * h, :]], axis=0).astype(BF16)
-        for z in range(n_row // HALVES):
-            send_ref[h * (n_row // HALVES) + z, 2 * own : 2 * own + 16, :] = chunk
-    for i in range(n_row):
-        send_ref[i, 2 * own + 16 :, :] = bias_rows
+        for k in range(FAR):
+            base = 2 * own * k
+            send_ref[i, base : base + own, :] = sums[k * own : (k + 1) * own, :LANES]
+            send_ref[i, base + own : base + 2 * own, :] = sums[k * own : (k + 1) * own, LANES:]
+        send_ref[i, 2 * own * FAR : 2 * own * FAR + 32, :] = chunk
+        send_ref[i, 2 * own * FAR + 32 :, :] = bias_rows
+
+
+def merged_bias(rows):
+    bias = rows[:2, :] + rows[2:4, :]
+    return bias_block(jnp.concatenate([bias[:1, :], bias[1:, :]], axis=1))
+
+
+def middle_kernel(recv_ref, send_ref):
+    part = (recv_ref.shape[1] - 40) // FAR
+    total = recv_ref[0].astype(F32)
+    for i in range(1, recv_ref.shape[0]):
+        total += recv_ref[i].astype(F32)
+    base = part * FAR
+    chunk = total[base : base + 32, :].astype(BF16)
+    bias_rows = merged_bias(total[base + 32 :, :])
+    for k in range(FAR):
+        send_ref[k, :part, :] = total[k * part : (k + 1) * part, :].astype(BF16)
+        send_ref[k, part : part + 32, :] = chunk
+        send_ref[k, part + 32 :, :] = bias_rows
 
 
 def final_kernel(recv_ref, feature_ref, bias_ref, spread_ref):
-    n_row, own = recv_ref.shape[0], feature_ref.shape[0]
+    own = feature_ref.shape[0]
     total = recv_ref[0].astype(F32)
-    for i in range(1, n_row):
+    for i in range(1, recv_ref.shape[0]):
         total += recv_ref[i].astype(F32)
     feature_ref[:, :LANES] = total[:own, :].astype(BF16)
     feature_ref[:, LANES:] = total[own : 2 * own, :].astype(BF16)
     base = 2 * own
-    chunk = jnp.concatenate([total[base : base + 8, :], total[base + 8 : base + 16, :]], axis=1)
     for i in range(spread_ref.shape[0]):
-        spread_ref[i] = chunk
-    bias = total[base + 16 : base + 18, :] + total[base + 18 : base + 20, :]
+        spread_ref[i, :, :LANES] = total[base : base + 16, :]
+        spread_ref[i, :, LANES:] = total[base + 16 : base + 32, :]
+    bias = total[base + 32 : base + 34, :] + total[base + 34 : base + 36, :]
     bias_ref[:, :LANES] = bias[:1, :]
     bias_ref[:, LANES:] = bias[1:, :]
 
@@ -175,7 +196,8 @@
 
 
 def make_body(n_row, n_col):
-    row_axes = ("half", "rest")
+    near_axes = ("half", "near")
+    n_near = HALVES * NEAR
 
     def body(
         features,
@@ -192,8 +214,10 @@
         size = n_row * own
         rows = cotangent.shape[0]
         shape = jax.ShapeDtypeStruct
-        sends = call(spread_kernel, shape((n_row, own, width), BF16), [VMEM])(features)
-        gathered = exchange(sends, row_axes).reshape(size, width)
+        sends = call(spread_kernel, shape((FAR, own, width), BF16), [VMEM])(features)
+        some = exchange(sends, "far")
+        sends = call(spread_kernel, shape((n_near, FAR * own, width), BF16), [VMEM])(some)
+        gathered = exchange(sends, near_axes).reshape(size, width)
         matrix, matrix_t, degree = call(
             edges_kernel,
             (shape((size, size), BF16), shape((size, size), BF16), shape((8, size), BF16)),
@@ -214,21 +238,23 @@
         recv_grads = exchange(send_grads, "col")
         send_back = call(
             backward_kernel,
-            shape((n_row, 2 * own + 24, LANES), BF16),
+            shape((n_near, 2 * own * FAR + 40, LANES), BF16),
             [VMEM] * 2,
             [pltpu.VMEM((size, width), BF16)],
         )(matrix_t, recv_grads)
-        recv_back = exchange(send_back, row_axes)
+        recv_near = exchange(send_back, near_axes)
+        send_far = call(middle_kernel, shape((FAR, 2 * own + 40, LANES), BF16), [VMEM])(recv_near)
+        recv_back = exchange(send_far, "far")
         feature_grad, bias_grad, send_weight = call(
             final_kernel,
             (
                 shape((own, width), BF16),
                 shape((1, width), F32),
-                shape((HALVES * n_col, 8, width), F32),
+                shape((n_col, 16, width), F32),
             ),
             [VMEM],
         )(recv_back)
-        weight_grad = exchange(send_weight, ("half", "col")).reshape(width, width)
+        weight_grad = exchange(send_weight, "col").reshape(width, width)
         return (output, feature_grad[None], weight_grad, bias_grad.reshape(width))
 
     return body
@@ -236,8 +262,8 @@
 
 def solution(mesh):
     n_row, n_col = mesh.shape["row"], mesh.shape["col"]
-    row = ("half", "rest")
-    split = Mesh(mesh.devices.reshape(HALVES, n_row // HALVES, n_col), row + ("col",))
+    row = ("half", "far", "near")
+    split = Mesh(mesh.devices.reshape(HALVES, FAR, NEAR, n_col), row + ("col",))
     return jax.shard_map(
         make_body(n_row, n_col),
         mesh=split,

time: 149 us -> 132 us (0.89)
  waiting for transfers between devices: 31 us -> 10.2 us
  blocking collectives: 73.2 us -> 92.3 us
  starting transfers between devices: 24.7 us -> 13.1 us
  local copies, waits for them, and re-layouts: 5.98 us -> 3.98 us
    all_to_all x2, waiting for transfers between devices: 31 us -> 10.2 us  [exchange(): return lax.all_to_all(blocks, axes, split_axis=0, concat_axis=0, tiled=True)]
    all_to_all x3 -> x5, blocking collectives: 73.2 us -> 92.3 us  [exchange(): return lax.all_to_all(blocks, axes, split_axis=0, concat_axis=0, tiled=True)]
    all_to_all x2, starting transfers between devices: 24.7 us -> 13.1 us  [exchange(): return lax.all_to_all(blocks, axes, split_axis=0, concat_axis=0, tiled=True)]
    unnamed x21, local copies, waits for them, and re-layouts: 5.98 us -> 3.98 us
  transfers between devices with their start and end apart: 2 -> 2, of which waited for: 2 -> 1; matrix products, arithmetic and copies ran while one was open for 0% -> 0% of each run, Pallas kernels for 4% -> 4%
where the time goes in v3:
time: 132 us
  blocking collectives  92.3 us (70%)
  starting transfers between devices  13.1 us (10%)
  Pallas kernels  10.5 us (8%)
  waiting for transfers between devices  10.2 us (8%)
  local copies, waits for them, and re-layouts  3.98 us (3%)
  between operations  1.37 us (1%)
    all_to_all x5, blocking collectives, exchange(): return lax.all_to_all(blocks, axes, split_axis=0, concat_axis=0, tiled=True)  92.3 us
    all_to_all x2, starting transfers between devices, exchange(): return lax.all_to_all(blocks, axes, split_axis=0, concat_axis=0, tiled=True)  13.1 us
    all_to_all x2, waiting for transfers between devices, exchange(): return lax.all_to_all(blocks, axes, split_axis=0, concat_axis=0, tiled=True)  10.2 us
    pallas_call x1, Pallas kernels, body(): call(edges_kernel, (shape((size, size), BF16), shape((size, size), BF16),...  5.82 us
    unnamed x21, local copies, waits for them, and re-layouts  3.98 us
  transfers between devices with their start and end apart: 2, of which 1 were waited for; matrix products, arithmetic and copies ran while one was open for 0% of the time, Pallas kernels for 4%

profile of v3, /device:TPU:1, one launch (start us, length us, event | category | flops | bytes accessed | tf_op | source)
XLA Modules:
  0.0 131.6 jit_solution(4639188629055450913)
XLA Ops:
  0.6 0.0 copy-start.4
  0.6 0.7 copy-done.4
  1.4 0.0 copy-start.7
  1.4 0.0 copy-start.8
  1.4 0.0 copy-start.9
  1.4 28.7 %all_to_all.35.block_ref = bf16[8,32,256]{2,1,0:T(8,128)(2,1)S(1)} all-to-all(bf16[8,32,256]{2,1,0:T(8,128)(2,1)S(1)} %spread_kernel.2), channel_id=1, replica_groups=mesh['half'=2,'far'=8,'near'=2,'col'=16] {'far'}, dimensions={0} | all-to-all | bytes 262144 | tf_op jit(solution)/shard_map/all_to_all | solution.py:181
  30.0 0.9 spread_kernel.3
  30.9 5.4 %all-to-all-start.1 = ((bf16[4,256,256]{2,1,0:T(8,128)(2,1)}), bf16[4,256,256]{2,1,0:T(8,128)(2,1)S(1)}, u32[]{:S(2)}, u32[]{:S(2)}) async-start(bf16[4,256,256]{2,1,0:T(8,128)(2,1)} %spread_kernel.3), calls=%async_computation.1 | async-start | bytes 1048576 | tf_op jit(solution)/shard_map/all_to_all | solution.py:181
  36.9 0.0 copy-done.7
  36.9 0.0 copy-done.8
  36.9 0.0 copy-done.9
  37.0 0.0 copy-start.6
  37.0 1.2 copy-done.6
  38.2 5.8 %edges_kernel.1 = (bf16[1024,1024]{1,0:T(8,128)(2,1)S(1)}, bf16[1024,1024]{1,0:T(8,128)(2,1)S(1)}, bf16[8,1024]{1,0:T(8,128)(2,1)S(1)}) custom-call(s32[1]{0:T(128)S(6)} %copy.14.count_ref, s32[32]{0:T(128)S(1)} %copy-done.8, s32[32]{0:T(128)S(1)} %copy-done.9, s32[1,1024]{1,0:T(1,128)S(1)} %copy-done.7, bf16[32,128,128]{2,1,0:T(8,128)(2,1)S(1)} %copy-done.6), custom_call_target="tpu_custom_call" | custom-call | flops 8589934592 | bytes 5242880 | tf_op jit(solution)/shard_map/edges_kernel/pallas_call | solution.py:221
  44.0 0.0 copy-start
  44.0 1.3 %copy-done = bf16[1024,1024]{1,0:T(8,128)(2,1)} copy-done((bf16[1024,1024]{1,0:T(8,128)(2,1)}, bf16[1024,1024]{1,0:T(8,128)(2,1)S(1)}, u32[]{:S(2)}) %copy-start) | copy-done | bytes 2097176
  45.3 0.0 all-to-all-done.1
  45.3 0.0 copy-start.2
  45.4 0.0 copy-start.3
  45.4 0.0 copy-start.5
  45.4 1.5 %forward_kernel.1 = bf16[16,136,128]{2,1,0:T(8,128)(2,1)} custom-call(bf16[1024,1024]{1,0:T(8,128)(2,1)S(1)} %get-tuple-element.12.m_ref, bf16[1024,256]{1,0:T(8,128)(2,1)S(1)} %bitcast.6, bf16[8,1024]{1,0:T(8,128)(2,1)S(1)} %get-tuple-element.13.deg_ref), custom_call_target="tpu_custom_call" | custom-call | tf_op jit(solution)/shard_map/forward_kernel/pallas_call | solution.py:228
  46.9 0.0 copy-start.1
  46.9 7.8 %all-to-all-start.2 = ((bf16[16,136,128]{2,1,0:T(8,128)(2,1)}), bf16[16,136,128]{2,1,0:T(8,128)(2,1)S(1)}, u32[]{:S(2)}, u32[]{:S(2)}) async-start(bf16[16,136,128]{2,1,0:T(8,128)(2,1)} %forward_kernel.1), calls=%async_computation.2 | async-start | bytes 1114112 | tf_op jit(solution)/shard_map/all_to_all | solution.py:181
  54.7 10.2 %all-to-all-done.2.recv_ref = bf16[16,136,128]{2,1,0:T(8,128)(2,1)S(1)} async-done(((bf16[16,136,128]{2,1,0:T(8,128)(2,1)}), bf16[16,136,128]{2,1,0:T(8,128)(2,1)S(1)}, u32[]{:S(2)}, u32[]{:S(2)}) %all-to-all-start.2) | async-done | bytes 557088 | tf_op jit(solution)/shard_map/all_to_all | solution.py:181
  64.9 0.0 copy-done.2
  64.9 0.0 copy-done.3
  64.9 0.0 copy-done.5
  64.9 0.9 dense_kernel.1
  65.8 15.5 %all_to_all.36.recv_ref = bf16[16,168,128]{2,1,0:T(8,128)(2,1)S(1)} all-to-all(bf16[16,168,128]{2,1,0:T(8,128)(2,1)S(1)} %get-tuple-element.16), channel_id=1, replica_groups=mesh['half'=2,'far'=8,'near'=2,'col'=16] {'col'}, dimensions={0} | all-to-all | bytes 1376256 | tf_op jit(solution)/shard_map/all_to_all | solution.py:181
  81.3 0.0 copy-done.1
  81.3 0.7 backward_kernel.1
  82.1 15.7 %all_to_all.37.recv_ref = bf16[4,552,128]{2,1,0:T(8,128)(2,1)S(1)} all-to-all(bf16[4,552,128]{2,1,0:T(8,128)(2,1)S(1)} %backward_kernel.1), channel_id=1, replica_groups=mesh['half'=2,'far'=8,'near'=2,'col'=16] {'half','near'}, dimensions={0} | all-to-all | bytes 1130496 | tf_op jit(solution)/shard_map/all_to_all | solution.py:181
  97.7 0.1 middle_kernel.1
  97.8 19.0 %all_to_all.38.recv_ref = bf16[8,104,128]{2,1,0:T(8,128)(2,1)S(1)} all-to-all(bf16[8,104,128]{2,1,0:T(8,128)(2,1)S(1)} %middle_kernel.1), channel_id=1, replica_groups=mesh['half'=2,'far'=8,'near'=2,'col'=16] {'far'}, dimensions={0} | all-to-all | bytes 425984 | tf_op jit(solution)/shard_map/all_to_all | solution.py:181
  116.8 0.6 final_kernel.1
  117.4 13.4 %all_to_all.39 = f32[16,16,256]{2,1,0:T(8,128)S(1)} all-to-all(f32[16,16,256]{2,1,0:T(8,128)S(1)} %get-tuple-element.18), channel_id=1, replica_groups=mesh['half'=2,'far'=8,'near'=2,'col'=16] {'col'}, dimensions={0} | all-to-all | bytes 524288 | tf_op jit(solution)/shard_map/all_to_all | solution.py:181
  130.9 0.7 copy.15
  (1 shorter events, 0.0 us)
Async XLA Ops:
  0.6 0.7 copy-start.4
  1.4 35.6 %copy-start.7 = (s32[1,1024]{1,0:T(1,128)S(1)}, s32[1,1024]{1,0:T(1,128)}, u32[]{:S(2)}) copy-start(s32[1,1024]{1,0:T(1,128)} %order_ref.1) | copy-start | bytes 12292
  1.4 35.6 %copy-start.8 = (s32[32]{0:T(128)S(1)}, s32[32]{0:T(128)}, u32[]{:S(2)}) copy-start(s32[32]{0:T(128)} %rows_ref.1) | copy-start | bytes 388
  1.4 35.6 %copy-start.9 = (s32[32]{0:T(128)S(1)}, s32[32]{0:T(128)}, u32[]{:S(2)}) copy-start(s32[32]{0:T(128)} %cols_ref.1) | copy-start | bytes 388
  30.9 14.4 %all-to-all-start.1 = ((bf16[4,256,256]{2,1,0:T(8,128)(2,1)}), bf16[4,256,256]{2,1,0:T(8,128)(2,1)S(1)}, u32[]{:S(2)}, u32[]{:S(2)}) async-start(bf16[4,256,256]{2,1,0:T(8,128)(2,1)} %spread_kernel.3), calls=%async_computation.1 | async-start | bytes 1048576 | tf_op jit(solution)/shard_map/all_to_all | solution.py:181
  37.0 1.2 copy-start.6
  44.0 1.3 %copy-start = (bf16[1024,1024]{1,0:T(8,128)(2,1)}, bf16[1024,1024]{1,0:T(8,128)(2,1)S(1)}, u32[]{:S(2)}) copy-start(bf16[1024,1024]{1,0:T(8,128)(2,1)S(1)} %get-tuple-element.15.mt_ref) | copy-start | bytes 6291460
  45.3 19.6 %copy-start.2 = (bf16[256,256]{1,0:T(8,128)(2,1)S(1)}, bf16[256,256]{1,0:T(8,128)(2,1)}, u32[]{:S(2)}) copy-start(bf16[256,256]{1,0:T(8,128)(2,1)} %weight_ref.1) | copy-start | bytes 393220
  45.4 19.6 %copy-start.3 = (bf16[64,256]{1,0:T(8,128)(2,1)S(1)}, bf16[64,256]{1,0:T(8,128)(2,1)}, u32[]{:S(2)}) copy-start(bf16[64,256]{1,0:T(8,128)(2,1)} %cot_ref.1) | copy-start | bytes 98308
  45.4 19.6 %copy-start.5 = (f32[256]{0:T(256)S(1)}, f32[256]{0:T(256)}, u32[]{:S(2)}) copy-start(f32[256]{0:T(256)} %param.16) | copy-start | bytes 3076
  46.9 34.4 %copy-start.1 = (bf16[1024,1024]{1,0:T(8,128)(2,1)S(1)}, bf16[1024,1024]{1,0:T(8,128)(2,1)}, u32[]{:S(2)}) copy-start(bf16[1024,1024]{1,0:T(8,128)(2,1)} %copy-done) | copy-start | bytes 6291460
  46.9 18.0 %all-to-all-start.2 = ((bf16[16,136,128]{2,1,0:T(8,128)(2,1)}), bf16[16,136,128]{2,1,0:T(8,128)(2,1)S(1)}, u32[]{:S(2)}, u32[]{:S(2)}) async-start(bf16[16,136,128]{2,1,0:T(8,128)(2,1)} %forward_kernel.1), calls=%async_computation.2 | async-start | bytes 1114112 | tf_op jit(solution)/shard_map/all_to_all | solution.py:181

commit v4 on v3

--- a/solution.py
+++ b/solution.py
@@ -13,7 +13,6 @@
 TN = (((0,), (0,)), ((), ()))
 VMEM = pl.BlockSpec(memory_space=pltpu.VMEM)
 SMEM = pl.BlockSpec(memory_space=pltpu.SMEM)
-PARAMS = pltpu.CompilerParams(vmem_limit_bytes=32 * 1024 * 1024)
 
 
 def dot_nt(left, right):
@@ -46,7 +45,7 @@
     return ((half * NEAR + near) * FAR + far) * own + low
 
 
-def edges_kernel(count_ref, rows_ref, cols_ref, order_ref, tiles_ref, m_ref, mt_ref, deg_ref, a_ref, p_ref):
+def edges_kernel(count_ref, rows_ref, cols_ref, order_ref, tiles_ref, m_ref, deg_ref, a_ref, p_ref):
     a_ref[...] = jnp.zeros_like(a_ref)
     tile = tiles_ref.shape[1]
 
@@ -66,11 +65,17 @@
     for start in range(0, size, step):
         part = slice(start, start + step)
         m_ref[:, part] = dot_nt(a_ref[...], p_ref[part, :]).astype(BF16)
-        mt_ref[:, part] = dot_nt(p_ref[...], a_ref[part, :]).astype(BF16)
     degree = dot_nt(jnp.ones((16, size), BF16), a_ref[...])[:8, :]
     high = jnp.floor(degree * (1.0 / 128.0))
     index = lax.broadcasted_iota(jnp.int32, degree.shape, 0)
-    deg_ref[...] = jnp.where(index == 0, high, degree - 128.0 * high).astype(BF16)
+    pairs = jnp.where(index == 0, high, degree - 128.0 * high)
+    rows = size * LANES // deg_ref.shape[1]
+    for j in range(size // rows):
+        block = pairs[:, j * rows // LANES * LANES :][:, :LANES]
+        first = j * rows % LANES
+        if first:
+            block = jnp.concatenate([block[:, first:], block[:, :first]], axis=1)
+        deg_ref[:, j * LANES : (j + 1) * LANES] = block.astype(BF16)
 
 
 def forward_kernel(m_ref, features_ref, deg_ref, send_ref):
@@ -85,11 +90,10 @@
             send_ref[start + k, :rows, :] = sums[k * rows : (k + 1) * rows, :LANES]
             send_ref[start + k, rows : 2 * rows, :] = sums[k * rows : (k + 1) * rows, LANES:]
     for j in range(n_col):
-        base = j * rows // LANES * LANES
-        send_ref[j, 2 * rows :, :] = deg_ref[:, base : base + LANES]
-
-
-def dense_kernel(half_ref, recv_ref, weight_ref, bias_ref, cot_ref, out_ref, send_ref):
+        send_ref[j, 2 * rows :, :] = deg_ref[:, j * LANES : (j + 1) * LANES]
+
+
+def dense_kernel(recv_ref, weight_ref, bias_ref, cot_ref, out_ref, send_ref):
     n_col, rows = recv_ref.shape[0], cot_ref.shape[0]
     total = recv_ref[0].astype(F32)
     for j in range(1, n_col):
@@ -97,7 +101,7 @@
     sums = jnp.concatenate([total[:rows, :], total[rows : 2 * rows, :]], axis=1)
     deg_lanes = 128.0 * total[2 * rows : 2 * rows + 1, :] + total[2 * rows + 1 : 2 * rows + 2, :]
     lane = lax.broadcasted_iota(jnp.int32, (rows, LANES), 1)
-    own = lax.broadcasted_iota(jnp.int32, (rows, LANES), 0) + rows * half_ref[0]
+    own = lax.broadcasted_iota(jnp.int32, (rows, LANES), 0)
     degree = jnp.sum(jnp.where(lane == own, deg_lanes, 0.0), axis=1, keepdims=True)
     scale = lax.rsqrt(jnp.maximum(degree, 1.0))
     agg = (sums * scale).astype(BF16)
@@ -118,9 +122,9 @@
         send_ref[j, 2 * rows + 32 :, :] = bias_rows
 
 
-def backward_kernel(mt_ref, recv_ref, send_ref, grads_ref):
+def backward_kernel(m_ref, recv_ref, send_ref, grads_ref):
     n_col, n_near = recv_ref.shape[0], send_ref.shape[0]
-    size = mt_ref.shape[0]
+    size, width = m_ref.shape[0], grads_ref.shape[1]
     rows, own = size // n_col, size // (n_near * FAR)
     extra = recv_ref[0, 2 * rows :, :].astype(F32)
     for j in range(1, n_col):
@@ -130,10 +134,13 @@
     for j in range(n_col):
         grads_ref[j * rows : (j + 1) * rows, :LANES] = recv_ref[j, :rows, :]
         grads_ref[j * rows : (j + 1) * rows, LANES:] = recv_ref[j, rows : 2 * rows, :]
+    index = lax.broadcasted_iota(jnp.int32, (width, width), 0)
+    unit = jnp.where(index == lax.broadcasted_iota(jnp.int32, (width, width), 1), 1.0, 0.0).astype(BF16)
+    turned = dot_nt(unit, grads_ref[...]).astype(BF16)
     for i in range(n_near):
-        sums = jnp.dot(
-            mt_ref[i * FAR * own : (i + 1) * FAR * own, :], grads_ref[...], preferred_element_type=F32
-        ).astype(BF16)
+        part = m_ref[:, i * FAR * own : (i + 1) * FAR * own]
+        sums = jnp.dot(turned, part, preferred_element_type=F32).astype(BF16)
+        sums = lax.dot_general(unit, sums, NT, preferred_element_type=F32).astype(BF16)
         for k in range(FAR):
             base = 2 * own * k
             send_ref[i, base : base + own, :] = sums[k * own : (k + 1) * own, :LANES]
@@ -181,7 +188,7 @@
     return lax.all_to_all(blocks, axes, split_axis=0, concat_axis=0, tiled=True)
 
 
-def call(kernel, out_shape, in_specs, scratch=(), **options):
+def call(kernel, out_shape, in_specs, scratch=(), vmem=8, **options):
     several = isinstance(out_shape, tuple)
     return pl.pallas_call(
         kernel,
@@ -189,7 +196,7 @@
         in_specs=in_specs,
         out_specs=(VMEM,) * len(out_shape) if several else VMEM,
         scratch_shapes=list(scratch),
-        compiler_params=PARAMS,
+        compiler_params=pltpu.CompilerParams(vmem_limit_bytes=vmem * 2**20),
         name=kernel.__name__,
         **options,
     )
@@ -216,32 +223,32 @@
         shape = jax.ShapeDtypeStruct
         sends = call(spread_kernel, shape((FAR, own, width), BF16), [VMEM])(features)
         some = exchange(sends, "far")
+        matrix, degree = call(
+            edges_kernel,
+            (shape((size, size), BF16), shape((8, n_col * LANES), BF16)),
+            [SMEM, SMEM, SMEM, VMEM, VMEM],
+            [pltpu.VMEM((size, size), BF16), pltpu.VMEM((size, size), BF16)],
+            vmem=12,
+            cost_estimate=pl.CostEstimate(flops=4 * size**3, bytes_accessed=3 * 2**20, transcendentals=0),
+        )(tile_count, tile_rows, tile_cols, node_order, tile_weights)
         sends = call(spread_kernel, shape((n_near, FAR * own, width), BF16), [VMEM])(some)
         gathered = exchange(sends, near_axes).reshape(size, width)
-        matrix, matrix_t, degree = call(
-            edges_kernel,
-            (shape((size, size), BF16), shape((size, size), BF16), shape((8, size), BF16)),
-            [SMEM, SMEM, SMEM, VMEM, VMEM],
-            [pltpu.VMEM((size, size), BF16), pltpu.VMEM((size, size), BF16)],
-            cost_estimate=pl.CostEstimate(flops=8 * size**3, bytes_accessed=5 * 2**20, transcendentals=0),
-        )(tile_count, tile_rows, tile_cols, node_order, tile_weights)
         send_sums = call(forward_kernel, shape((n_col, 2 * rows + 8, LANES), BF16), [VMEM] * 3)(
             matrix, gathered, degree
         )
         recv_sums = exchange(send_sums, "col")
-        half = (lax.axis_index("col") * rows % LANES // rows).astype(jnp.int32).reshape(1)
         output, send_grads = call(
             dense_kernel,
             (shape((rows, width), BF16), shape((n_col, 2 * rows + 40, LANES), BF16)),
-            [SMEM] + [VMEM] * 4,
-        )(half, recv_sums, weight, bias_vector.reshape(1, width), cotangent)
+            [VMEM] * 4,
+        )(recv_sums, weight, bias_vector.reshape(1, width), cotangent)
         recv_grads = exchange(send_grads, "col")
         send_back = call(
             backward_kernel,
             shape((n_near, 2 * own * FAR + 40, LANES), BF16),
             [VMEM] * 2,
             [pltpu.VMEM((size, width), BF16)],
-        )(matrix_t, recv_grads)
+        )(matrix, recv_grads)
         recv_near = exchange(send_back, near_axes)
         send_far = call(middle_kernel, shape((FAR, 2 * own + 40, LANES), BF16), [VMEM])(recv_near)
         recv_back = exchange(send_far, "far")

time: 132 us -> 129 us (0.977)
  blocking collectives: 92.3 us -> 109 us
  waiting for transfers between devices: 10.2 us -> 0.92 us
  starting transfers between devices: 13.1 us -> 5.37 us
    all_to_all x5 -> x6, blocking collectives: 92.3 us -> 109 us  [exchange(): return lax.all_to_all(blocks, axes, split_axis=0, concat_axis=0, tiled=True)]
    all_to_all x2 -> x1, waiting for transfers between devices: 10.2 us -> 0.92 us  [exchange(): return lax.all_to_all(blocks, axes, split_axis=0, concat_axis=0, tiled=True)]
    all_to_all x2 -> x1, starting transfers between devices: 13.1 us -> 5.37 us  [exchange(): return lax.all_to_all(blocks, axes, split_axis=0, concat_axis=0, tiled=True)]
    pallas_call x1, Pallas kernels: 5.82 us -> 4.11 us  [body(): call(edges_kernel, (shape((size, size), BF16), shape((8, n_col * LANES),...]
    pallas_call x1, Pallas kernels: 0.73 us -> 2.19 us  [body(): call(backward_kernel, shape((n_near, 2 * own * FAR + 40, LANES), BF16), [...]
    unnamed x21 -> x17, local copies, waits for them, and re-layouts: 3.98 us -> 2.66 us
  transfers between devices with their start and end apart: 2 -> 1, of which waited for: 1 -> 1; matrix products, arithmetic and copies ran while one was open for 0% -> 0% of each run, Pallas kernels for 4% -> 3%
where the time goes in v4:
time: 129 us
  blocking collectives  109 us (84%)
  Pallas kernels  9.44 us (7%)
  starting transfers between devices  5.37 us (4%)
  local copies, waits for them, and re-layouts  2.66 us (2%)
  between operations  1.36 us (1%)
    all_to_all x6, blocking collectives, exchange(): return lax.all_to_all(blocks, axes, split_axis=0, concat_axis=0, tiled=True)  109 us
    all_to_all x1, starting transfers between devices, exchange(): return lax.all_to_all(blocks, axes, split_axis=0, concat_axis=0, tiled=True)  5.37 us
    pallas_call x1, Pallas kernels, body(): call(edges_kernel, (shape((size, size), BF16), shape((8, n_col * LANES),...  4.11 us
    unnamed x17, local copies, waits for them, and re-layouts  2.66 us
  transfers between devices with their start and end apart: 1, of which 1 were waited for; matrix products, arithmetic and copies ran while one was open for 0% of the time, Pallas kernels for 3%

profile of v4, /device:TPU:1, one launch (start us, length us, event | category | flops | bytes accessed | tf_op | source)
XLA Modules:
  0.0 128.6 jit_solution(12887072588047196605)
XLA Ops:
  0.6 0.0 copy-start.2
  0.6 0.7 copy-done.2
  1.4 0.0 copy-start.5
  1.4 0.0 copy-start.6
  1.4 0.0 copy-start.7
  1.4 28.7 %all_to_all.35.block_ref = bf16[8,32,256]{2,1,0:T(8,128)(2,1)S(1)} all-to-all(bf16[8,32,256]{2,1,0:T(8,128)(2,1)S(1)} %spread_kernel.2), channel_id=1, replica_groups=mesh['half'=2,'far'=8,'near'=2,'col'=16] {'far'}, dimensions={0} | all-to-all | bytes 262144 | tf_op jit(solution)/shard_map/all_to_all | solution.py:188
  30.0 0.8 spread_kernel.3
  30.9 5.4 %all-to-all-start.1 = ((bf16[4,256,256]{2,1,0:T(8,128)(2,1)}), bf16[4,256,256]{2,1,0:T(8,128)(2,1)S(1)}, u32[]{:S(2)}, u32[]{:S(2)}) async-start(bf16[4,256,256]{2,1,0:T(8,128)(2,1)} %spread_kernel.3), calls=%async_computation.1 | async-start | bytes 1048576 | tf_op jit(solution)/shard_map/all_to_all | solution.py:188
  36.9 0.0 copy-done.5
  36.9 0.0 copy-done.6
  36.9 0.0 copy-done.7
  36.9 0.0 copy-start.4
  37.0 1.2 copy-done.4
  38.2 4.1 %edges_kernel.1 = (bf16[1024,1024]{1,0:T(8,128)(2,1)S(1)}, bf16[8,2048]{1,0:T(8,128)(2,1)S(1)}) custom-call(s32[1]{0:T(128)S(6)} %copy.14.count_ref, s32[32]{0:T(128)S(1)} %copy-done.6, s32[32]{0:T(128)S(1)} %copy-done.7, s32[1,1024]{1,0:T(1,128)S(1)} %copy-done.5, bf16[32,128,128]{2,1,0:T(8,128)(2,1)S(1)} %copy-done.4), custom_call_target="tpu_custom_call" | custom-call | flops 4294967296 | bytes 3145728 | tf_op jit(solution)/shard_map/edges_kernel/pallas_call | solution.py:226
  42.3 0.9 all-to-all-done.1
  43.2 0.0 copy-start
  43.2 0.0 copy-start.1
  43.2 0.0 copy-start.3
  43.2 0.7 forward_kernel.1
  43.9 19.6 %all_to_all.36.recv_ref = bf16[16,136,128]{2,1,0:T(8,128)(2,1)S(1)} all-to-all(bf16[16,136,128]{2,1,0:T(8,128)(2,1)S(1)} %forward_kernel.1), channel_id=1, replica_groups=mesh['half'=2,'far'=8,'near'=2,'col'=16] {'col'}, dimensions={0} | all-to-all | bytes 1114112 | tf_op jit(solution)/shard_map/all_to_all | solution.py:188
  63.5 0.0 copy-done
  63.5 0.0 copy-done.1
  63.5 0.0 copy-done.3
  63.5 0.9 dense_kernel.1
  64.4 14.8 %all_to_all.37.recv_ref = bf16[16,168,128]{2,1,0:T(8,128)(2,1)S(1)} all-to-all(bf16[16,168,128]{2,1,0:T(8,128)(2,1)S(1)} %get-tuple-element.14), channel_id=1, replica_groups=mesh['half'=2,'far'=8,'near'=2,'col'=16] {'col'}, dimensions={0} | all-to-all | bytes 1376256 | tf_op jit(solution)/shard_map/all_to_all | solution.py:188
  79.3 2.2 %backward_kernel.1 = bf16[4,552,128]{2,1,0:T(8,128)(2,1)S(1)} custom-call(bf16[1024,1024]{1,0:T(8,128)(2,1)S(1)} %get-tuple-element.11.m_ref, bf16[16,168,128]{2,1,0:T(8,128)(2,1)S(1)} %all_to_all.37.recv_ref), custom_call_target="tpu_custom_call" | custom-call | tf_op jit(solution)/shard_map/backward_kernel/pallas_call | solution.py:246
  81.5 13.3 %all_to_all.38.recv_ref = bf16[4,552,128]{2,1,0:T(8,128)(2,1)S(1)} all-to-all(bf16[4,552,128]{2,1,0:T(8,128)(2,1)S(1)} %backward_kernel.1), channel_id=1, replica_groups=mesh['half'=2,'far'=8,'near'=2,'col'=16] {'half','near'}, dimensions={0} | all-to-all | bytes 1130496 | tf_op jit(solution)/shard_map/all_to_all | solution.py:188
  94.7 0.1 middle_kernel.1
  94.8 18.9 %all_to_all.39.recv_ref = bf16[8,104,128]{2,1,0:T(8,128)(2,1)S(1)} all-to-all(bf16[8,104,128]{2,1,0:T(8,128)(2,1)S(1)} %middle_kernel.1), channel_id=1, replica_groups=mesh['half'=2,'far'=8,'near'=2,'col'=16] {'far'}, dimensions={0} | all-to-all | bytes 425984 | tf_op jit(solution)/shard_map/all_to_all | solution.py:188
  113.7 0.6 final_kernel.1
  114.3 13.6 %all_to_all.40 = f32[16,16,256]{2,1,0:T(8,128)S(1)} all-to-all(f32[16,16,256]{2,1,0:T(8,128)S(1)} %get-tuple-element.16), channel_id=1, replica_groups=mesh['half'=2,'far'=8,'near'=2,'col'=16] {'col'}, dimensions={0} | all-to-all | bytes 524288 | tf_op jit(solution)/shard_map/all_to_all | solution.py:188
  127.9 0.7 copy.15
  (1 shorter events, 0.0 us)
Async XLA Ops:
  0.6 0.7 copy-start.2
  1.4 35.6 %copy-start.5 = (s32[1,1024]{1,0:T(1,128)S(1)}, s32[1,1024]{1,0:T(1,128)}, u32[]{:S(2)}) copy-start(s32[1,1024]{1,0:T(1,128)} %order_ref.1) | copy-start | bytes 12292
  1.4 35.6 %copy-start.6 = (s32[32]{0:T(128)S(1)}, s32[32]{0:T(128)}, u32[]{:S(2)}) copy-start(s32[32]{0:T(128)} %rows_ref.1) | copy-start | bytes 388
  1.4 35.6 %copy-start.7 = (s32[32]{0:T(128)S(1)}, s32[32]{0:T(128)}, u32[]{:S(2)}) copy-start(s32[32]{0:T(128)} %cols_ref.1) | copy-start | bytes 388
  30.9 12.3 %all-to-all-start.1 = ((bf16[4,256,256]{2,1,0:T(8,128)(2,1)}), bf16[4,256,256]{2,1,0:T(8,128)(2,1)S(1)}, u32[]{:S(2)}, u32[]{:S(2)}) async-start(bf16[4,256,256]{2,1,0:T(8,128)(2,1)} %spread_kernel.3), calls=%async_computation.1 | async-start | bytes 1048576 | tf_op jit(solution)/shard_map/all_to_all | solution.py:188
  36.9 1.2 copy-start.4
  43.2 20.3 %copy-start = (bf16[256,256]{1,0:T(8,128)(2,1)S(1)}, bf16[256,256]{1,0:T(8,128)(2,1)}, u32[]{:S(2)}) copy-start(bf16[256,256]{1,0:T(8,128)(2,1)} %weight_ref.1) | copy-start | bytes 393220
  43.2 20.3 %copy-start.1 = (bf16[64,256]{1,0:T(8,128)(2,1)S(1)}, bf16[64,256]{1,0:T(8,128)(2,1)}, u32[]{:S(2)}) copy-start(bf16[64,256]{1,0:T(8,128)(2,1)} %cot_ref.1) | copy-start | bytes 98308
  43.2 20.3 %copy-start.3 = (f32[256]{0:T(256)S(1)}, f32[256]{0:T(256)}, u32[]{:S(2)}) copy-start(f32[256]{0:T(256)} %param.16) | copy-start | bytes 3076

commit v5 on v4

--- a/solution.py
+++ b/solution.py
@@ -124,7 +124,7 @@
 
 def backward_kernel(m_ref, recv_ref, send_ref, grads_ref):
     n_col, n_near = recv_ref.shape[0], send_ref.shape[0]
-    size, width = m_ref.shape[0], grads_ref.shape[1]
+    size = m_ref.shape[0]
     rows, own = size // n_col, size // (n_near * FAR)
     extra = recv_ref[0, 2 * rows :, :].astype(F32)
     for j in range(1, n_col):
@@ -134,13 +134,9 @@
     for j in range(n_col):
         grads_ref[j * rows : (j + 1) * rows, :LANES] = recv_ref[j, :rows, :]
         grads_ref[j * rows : (j + 1) * rows, LANES:] = recv_ref[j, rows : 2 * rows, :]
-    index = lax.broadcasted_iota(jnp.int32, (width, width), 0)
-    unit = jnp.where(index == lax.broadcasted_iota(jnp.int32, (width, width), 1), 1.0, 0.0).astype(BF16)
-    turned = dot_nt(unit, grads_ref[...]).astype(BF16)
     for i in range(n_near):
         part = m_ref[:, i * FAR * own : (i + 1) * FAR * own]
-        sums = jnp.dot(turned, part, preferred_element_type=F32).astype(BF16)
-        sums = lax.dot_general(unit, sums, NT, preferred_element_type=F32).astype(BF16)
+        sums = lax.dot_general(part, grads_ref[...], TN, preferred_element_type=F32).astype(BF16)
         for k in range(FAR):
             base = 2 * own * k
             send_ref[i, base : base + own, :] = sums[k * own : (k + 1) * own, :LANES]

time: 129 us -> 128 us (level)
  Pallas kernels: 9.44 us -> 7.64 us
    pallas_call x1, Pallas kernels: 2.19 us -> 0.78 us  [body(): call(backward_kernel, shape((n_near, 2 * own * FAR + 40, LANES), BF16), [...]
where the time goes in v5:
time: 128 us; the launch traced here: 127 us
  blocking collectives  109 us (85%)
  Pallas kernels  7.64 us (6%)
  starting transfers between devices  5.37 us (4%)
  local copies, waits for them, and re-layouts  2.66 us (2%)
  between operations  1.36 us (1%)
  waiting for transfers between devices  1.31 us (1%)
    all_to_all x6, blocking collectives, exchange(): return lax.all_to_all(blocks, axes, split_axis=0, concat_axis=0, tiled=True)  109 us
    all_to_all x1, starting transfers between devices, exchange(): return lax.all_to_all(blocks, axes, split_axis=0, concat_axis=0, tiled=True)  5.37 us
    pallas_call x1, Pallas kernels, body(): call(edges_kernel, (shape((size, size), BF16), shape((8, n_col * LANES),...  3.71 us
    unnamed x17, local copies, waits for them, and re-layouts  2.66 us
  transfers between devices with their start and end apart: 1, of which 1 were waited for; matrix products, arithmetic and copies ran while one was open for 0% of the time, Pallas kernels for 3%

profile of v5, /device:TPU:1, one launch (start us, length us, event | category | flops | bytes accessed | tf_op | source)
XLA Modules:
  0.0 127.2 jit_solution(1378305439801935546)
XLA Ops:
  0.6 0.0 copy-start.2
  0.6 0.7 copy-done.2
  1.4 0.0 copy-start.5
  1.4 0.0 copy-start.6
  1.4 0.0 copy-start.7
  1.4 28.7 %all_to_all.35.block_ref = bf16[8,32,256]{2,1,0:T(8,128)(2,1)S(1)} all-to-all(bf16[8,32,256]{2,1,0:T(8,128)(2,1)S(1)} %spread_kernel.2), channel_id=1, replica_groups=mesh['half'=2,'far'=8,'near'=2,'col'=16] {'far'}, dimensions={0} | all-to-all | bytes 262144 | tf_op jit(solution)/shard_map/all_to_all | solution.py:184
  30.0 0.8 spread_kernel.3
  30.9 5.4 %all-to-all-start.1 = ((bf16[4,256,256]{2,1,0:T(8,128)(2,1)}), bf16[4,256,256]{2,1,0:T(8,128)(2,1)S(1)}, u32[]{:S(2)}, u32[]{:S(2)}) async-start(bf16[4,256,256]{2,1,0:T(8,128)(2,1)} %spread_kernel.3), calls=%async_computation.1 | async-start | bytes 1048576 | tf_op jit(solution)/shard_map/all_to_all | solution.py:184
  36.9 0.0 copy-done.5
  36.9 0.0 copy-done.6
  36.9 0.0 copy-done.7
  36.9 0.0 copy-start.4
  37.0 1.2 copy-done.4
  38.2 3.7 %edges_kernel.1 = (bf16[1024,1024]{1,0:T(8,128)(2,1)S(1)}, bf16[8,2048]{1,0:T(8,128)(2,1)S(1)}) custom-call(s32[1]{0:T(128)S(6)} %copy.14.count_ref, s32[32]{0:T(128)S(1)} %copy-done.6, s32[32]{0:T(128)S(1)} %copy-done.7, s32[1,1024]{1,0:T(1,128)S(1)} %copy-done.5, bf16[32,128,128]{2,1,0:T(8,128)(2,1)S(1)} %copy-done.4), custom_call_target="tpu_custom_call" | custom-call | flops 4294967296 | bytes 3145728 | tf_op jit(solution)/shard_map/edges_kernel/pallas_call | solution.py:222
  41.9 1.3 %all-to-all-done.1 = bf16[4,256,256]{2,1,0:T(8,128)(2,1)S(1)} async-done(((bf16[4,256,256]{2,1,0:T(8,128)(2,1)}), bf16[4,256,256]{2,1,0:T(8,128)(2,1)S(1)}, u32[]{:S(2)}, u32[]{:S(2)}) %all-to-all-start.1) | async-done | bytes 524320 | tf_op jit(solution)/shard_map/all_to_all | solution.py:184
  43.2 0.0 copy-start
  43.2 0.0 copy-start.1
  43.2 0.0 copy-start.3
  43.2 0.7 forward_kernel.1
  43.9 19.6 %all_to_all.36.recv_ref = bf16[16,136,128]{2,1,0:T(8,128)(2,1)S(1)} all-to-all(bf16[16,136,128]{2,1,0:T(8,128)(2,1)S(1)} %forward_kernel.1), channel_id=1, replica_groups=mesh['half'=2,'far'=8,'near'=2,'col'=16] {'col'}, dimensions={0} | all-to-all | bytes 1114112 | tf_op jit(solution)/shard_map/all_to_all | solution.py:184
  63.5 0.0 copy-done
  63.5 0.0 copy-done.1
  63.5 0.0 copy-done.3
  63.5 0.9 dense_kernel.1
  64.4 14.8 %all_to_all.37.recv_ref = bf16[16,168,128]{2,1,0:T(8,128)(2,1)S(1)} all-to-all(bf16[16,168,128]{2,1,0:T(8,128)(2,1)S(1)} %get-tuple-element.14), channel_id=1, replica_groups=mesh['half'=2,'far'=8,'near'=2,'col'=16] {'col'}, dimensions={0} | all-to-all | bytes 1376256 | tf_op jit(solution)/shard_map/all_to_all | solution.py:184
  79.3 0.8 backward_kernel.1
  80.1 13.3 %all_to_all.38.recv_ref = bf16[4,552,128]{2,1,0:T(8,128)(2,1)S(1)} all-to-all(bf16[4,552,128]{2,1,0:T(8,128)(2,1)S(1)} %backward_kernel.1), channel_id=1, replica_groups=mesh['half'=2,'far'=8,'near'=2,'col'=16] {'half','near'}, dimensions={0} | all-to-all | bytes 1130496 | tf_op jit(solution)/shard_map/all_to_all | solution.py:184
  93.3 0.1 middle_kernel.1
  93.4 18.9 %all_to_all.39.recv_ref = bf16[8,104,128]{2,1,0:T(8,128)(2,1)S(1)} all-to-all(bf16[8,104,128]{2,1,0:T(8,128)(2,1)S(1)} %middle_kernel.1), channel_id=1, replica_groups=mesh['half'=2,'far'=8,'near'=2,'col'=16] {'far'}, dimensions={0} | all-to-all | bytes 425984 | tf_op jit(solution)/shard_map/all_to_all | solution.py:184
  112.3 0.6 final_kernel.1
  112.9 13.6 %all_to_all.40 = f32[16,16,256]{2,1,0:T(8,128)S(1)} all-to-all(f32[16,16,256]{2,1,0:T(8,128)S(1)} %get-tuple-element.16), channel_id=1, replica_groups=mesh['half'=2,'far'=8,'near'=2,'col'=16] {'col'}, dimensions={0} | all-to-all | bytes 524288 | tf_op jit(solution)/shard_map/all_to_all | solution.py:184
  126.5 0.7 copy.15
  (1 shorter events, 0.0 us)
Async XLA Ops:
  0.6 0.7 copy-start.2
  1.4 35.6 %copy-start.5 = (s32[1,1024]{1,0:T(1,128)S(1)}, s32[1,1024]{1,0:T(1,128)}, u32[]{:S(2)}) copy-start(s32[1,1024]{1,0:T(1,128)} %order_ref.1) | copy-start | bytes 12292
  1.4 35.6 %copy-start.6 = (s32[32]{0:T(128)S(1)}, s32[32]{0:T(128)}, u32[]{:S(2)}) copy-start(s32[32]{0:T(128)} %rows_ref.1) | copy-start | bytes 388
  1.4 35.6 %copy-start.7 = (s32[32]{0:T(128)S(1)}, s32[32]{0:T(128)}, u32[]{:S(2)}) copy-start(s32[32]{0:T(128)} %cols_ref.1) | copy-start | bytes 388
  30.9 12.3 %all-to-all-start.1 = ((bf16[4,256,256]{2,1,0:T(8,128)(2,1)}), bf16[4,256,256]{2,1,0:T(8,128)(2,1)S(1)}, u32[]{:S(2)}, u32[]{:S(2)}) async-start(bf16[4,256,256]{2,1,0:T(8,128)(2,1)} %spread_kernel.3), calls=%async_computation.1 | async-start | bytes 1048576 | tf_op jit(solution)/shard_map/all_to_all | solution.py:184
  36.9 1.2 copy-start.4
  43.2 20.3 %copy-start = (bf16[256,256]{1,0:T(8,128)(2,1)S(1)}, bf16[256,256]{1,0:T(8,128)(2,1)}, u32[]{:S(2)}) copy-start(bf16[256,256]{1,0:T(8,128)(2,1)} %weight_ref.1) | copy-start | bytes 393220
  43.2 20.3 %copy-start.1 = (bf16[64,256]{1,0:T(8,128)(2,1)S(1)}, bf16[64,256]{1,0:T(8,128)(2,1)}, u32[]{:S(2)}) copy-start(bf16[64,256]{1,0:T(8,128)(2,1)} %cot_ref.1) | copy-start | bytes 98308
  43.2 20.3 %copy-start.3 = (f32[256]{0:T(256)S(1)}, f32[256]{0:T(256)}, u32[]{:S(2)}) copy-start(f32[256]{0:T(256)} %param.16) | copy-start | bytes 3076

commit v6 on v5

--- a/solution.py
+++ b/solution.py
@@ -164,20 +164,29 @@
         send_ref[k, part + 32 :, :] = bias_rows
 
 
-def final_kernel(recv_ref, feature_ref, bias_ref, spread_ref):
+def weight_kernel(recv_ref, spread_ref):
+    base = recv_ref.shape[1] - 40
+    total = recv_ref[0, base : base + 32, :].astype(F32)
+    for i in range(1, recv_ref.shape[0]):
+        total += recv_ref[i, base : base + 32, :].astype(F32)
+    for i in range(spread_ref.shape[0]):
+        spread_ref[i, :, :LANES] = total[:16, :]
+        spread_ref[i, :, LANES:] = total[16:, :]
+
+
+def store_kernel(recv_ref, chunks_ref, output_ref, feature_ref, bias_ref, weight_ref, out_ref):
     own = feature_ref.shape[0]
     total = recv_ref[0].astype(F32)
     for i in range(1, recv_ref.shape[0]):
         total += recv_ref[i].astype(F32)
     feature_ref[:, :LANES] = total[:own, :].astype(BF16)
     feature_ref[:, LANES:] = total[own : 2 * own, :].astype(BF16)
-    base = 2 * own
-    for i in range(spread_ref.shape[0]):
-        spread_ref[i, :, :LANES] = total[base : base + 16, :]
-        spread_ref[i, :, LANES:] = total[base + 16 : base + 32, :]
-    bias = total[base + 32 : base + 34, :] + total[base + 34 : base + 36, :]
+    base = 2 * own + 32
+    bias = total[base : base + 2, :] + total[base + 2 : base + 4, :]
     bias_ref[:, :LANES] = bias[:1, :]
     bias_ref[:, LANES:] = bias[1:, :]
+    weight_ref[...] = chunks_ref[...].reshape(weight_ref.shape)
+    out_ref[...] = output_ref[...]
 
 
 def exchange(blocks, axes):
@@ -248,16 +257,18 @@
         recv_near = exchange(send_back, near_axes)
         send_far = call(middle_kernel, shape((FAR, 2 * own + 40, LANES), BF16), [VMEM])(recv_near)
         recv_back = exchange(send_far, "far")
-        feature_grad, bias_grad, send_weight = call(
-            final_kernel,
+        send_weight = call(weight_kernel, shape((n_col, 16, width), F32), [VMEM])(recv_back)
+        chunks = exchange(send_weight, "col")
+        feature_grad, bias_grad, weight_grad, output = call(
+            store_kernel,
             (
                 shape((own, width), BF16),
                 shape((1, width), F32),
-                shape((n_col, 16, width), F32),
+                shape((width, width), F32),
+                shape((rows, width), BF16),
             ),
-            [VMEM],
-        )(recv_back)
-        weight_grad = exchange(send_weight, "col").reshape(width, width)
+            [VMEM] * 3,
+        )(recv_back, chunks, output)
         return (output, feature_grad[None], weight_grad, bias_grad.reshape(width))
 
     return body

time: 128 us -> 127 us (level)
    unnamed x17 -> x16, local copies, waits for them, and re-layouts: 2.66 us -> 1.95 us
where the time goes in v6:
time: 127 us; the launch traced here: 126 us
  blocking collectives  109 us (86%)
  Pallas kernels  7.31 us (6%)
  starting transfers between devices  5.37 us (4%)
  local copies, waits for them, and re-layouts  1.95 us (2%)
  between operations  1.37 us (1%)
  waiting for transfers between devices  1.31 us (1%)
    all_to_all x6, blocking collectives, exchange(): return lax.all_to_all(blocks, axes, split_axis=0, concat_axis=0, tiled=True)  109 us
    all_to_all x1, starting transfers between devices, exchange(): return lax.all_to_all(blocks, axes, split_axis=0, concat_axis=0, tiled=True)  5.37 us
    pallas_call x1, Pallas kernels, body(): call(edges_kernel, (shape((size, size), BF16), shape((8, n_col * LANES),...  3.71 us
  transfers between devices with their start and end apart: 1, of which 1 were waited for; matrix products, arithmetic and copies ran while one was open for 0% of the time, Pallas kernels for 3%

profile of v6, /device:TPU:1, one launch (start us, length us, event | category | flops | bytes accessed | tf_op | source)
XLA Modules:
  0.0 126.2 jit_solution(11193856588815056011)
XLA Ops:
  0.6 0.0 copy-start.2
  0.6 0.7 copy-done.2
  1.4 0.0 copy-start.5
  1.4 0.0 copy-start.6
  1.4 0.0 copy-start.7
  1.4 28.7 %all_to_all.35.block_ref = bf16[8,32,256]{2,1,0:T(8,128)(2,1)S(1)} all-to-all(bf16[8,32,256]{2,1,0:T(8,128)(2,1)S(1)} %spread_kernel.2), channel_id=1, replica_groups=mesh['half'=2,'far'=8,'near'=2,'col'=16] {'far'}, dimensions={0} | all-to-all | bytes 262144 | tf_op jit(solution)/shard_map/all_to_all | solution.py:193
  30.0 0.8 spread_kernel.3
  30.9 5.4 %all-to-all-start.1 = ((bf16[4,256,256]{2,1,0:T(8,128)(2,1)}), bf16[4,256,256]{2,1,0:T(8,128)(2,1)S(1)}, u32[]{:S(2)}, u32[]{:S(2)}) async-start(bf16[4,256,256]{2,1,0:T(8,128)(2,1)} %spread_kernel.3), calls=%async_computation.1 | async-start | bytes 1048576 | tf_op jit(solution)/shard_map/all_to_all | solution.py:193
  36.9 0.0 copy-done.5
  36.9 0.0 copy-done.6
  36.9 0.0 copy-done.7
  36.9 0.0 copy-start.4
  37.0 1.2 copy-done.4
  38.2 3.7 %edges_kernel.1 = (bf16[1024,1024]{1,0:T(8,128)(2,1)S(1)}, bf16[8,2048]{1,0:T(8,128)(2,1)S(1)}) custom-call(s32[1]{0:T(128)S(6)} %copy.13.count_ref, s32[32]{0:T(128)S(1)} %copy-done.6, s32[32]{0:T(128)S(1)} %copy-done.7, s32[1,1024]{1,0:T(1,128)S(1)} %copy-done.5, bf16[32,128,128]{2,1,0:T(8,128)(2,1)S(1)} %copy-done.4), custom_call_target="tpu_custom_call" | custom-call | flops 4294967296 | bytes 3145728 | tf_op jit(solution)/shard_map/edges_kernel/pallas_call | solution.py:231
  41.9 1.3 %all-to-all-done.1 = bf16[4,256,256]{2,1,0:T(8,128)(2,1)S(1)} async-done(((bf16[4,256,256]{2,1,0:T(8,128)(2,1)}), bf16[4,256,256]{2,1,0:T(8,128)(2,1)S(1)}, u32[]{:S(2)}, u32[]{:S(2)}) %all-to-all-start.1) | async-done | bytes 524320 | tf_op jit(solution)/shard_map/all_to_all | solution.py:193
  43.2 0.0 copy-start
  43.2 0.0 copy-start.1
  43.2 0.0 copy-start.3
  43.2 0.7 forward_kernel.1
  43.9 19.6 %all_to_all.36.recv_ref = bf16[16,136,128]{2,1,0:T(8,128)(2,1)S(1)} all-to-all(bf16[16,136,128]{2,1,0:T(8,128)(2,1)S(1)} %forward_kernel.1), channel_id=1, replica_groups=mesh['half'=2,'far'=8,'near'=2,'col'=16] {'col'}, dimensions={0} | all-to-all | bytes 1114112 | tf_op jit(solution)/shard_map/all_to_all | solution.py:193
  63.5 0.0 copy-done
  63.5 0.0 copy-done.1
  63.5 0.0 copy-done.3
  63.5 0.4 dense_kernel.1
  64.0 14.9 %all_to_all.37.recv_ref = bf16[16,168,128]{2,1,0:T(8,128)(2,1)S(1)} all-to-all(bf16[16,168,128]{2,1,0:T(8,128)(2,1)S(1)} %get-tuple-element.14), channel_id=1, replica_groups=mesh['half'=2,'far'=8,'near'=2,'col'=16] {'col'}, dimensions={0} | all-to-all | bytes 1376256 | tf_op jit(solution)/shard_map/all_to_all | solution.py:193
  78.8 0.8 backward_kernel.1
  79.6 13.3 %all_to_all.38.recv_ref = bf16[4,552,128]{2,1,0:T(8,128)(2,1)S(1)} all-to-all(bf16[4,552,128]{2,1,0:T(8,128)(2,1)S(1)} %backward_kernel.1), channel_id=1, replica_groups=mesh['half'=2,'far'=8,'near'=2,'col'=16] {'half','near'}, dimensions={0} | all-to-all | bytes 1130496 | tf_op jit(solution)/shard_map/all_to_all | solution.py:193
  92.9 0.1 middle_kernel.1
  93.0 18.8 %all_to_all.39.recv_ref = bf16[8,104,128]{2,1,0:T(8,128)(2,1)S(1)} all-to-all(bf16[8,104,128]{2,1,0:T(8,128)(2,1)S(1)} %middle_kernel.1), channel_id=1, replica_groups=mesh['half'=2,'far'=8,'near'=2,'col'=16] {'far'}, dimensions={0} | all-to-all | bytes 425984 | tf_op jit(solution)/shard_map/all_to_all | solution.py:193
  111.9 13.6 %all_to_all.40.chunks_ref = f32[16,16,256]{2,1,0:T(8,128)S(1)} all-to-all(f32[16,16,256]{2,1,0:T(8,128)S(1)} %weight_kernel.1), channel_id=1, replica_groups=mesh['half'=2,'far'=8,'near'=2,'col'=16] {'col'}, dimensions={0} | all-to-all | bytes 524288 | tf_op jit(solution)/shard_map/all_to_all | solution.py:193
  125.4 0.7 store_kernel.1
  (2 shorter events, 0.0 us)
Async XLA Ops:
  0.6 0.7 copy-start.2
  1.4 35.6 %copy-start.5 = (s32[1,1024]{1,0:T(1,128)S(1)}, s32[1,1024]{1,0:T(1,128)}, u32[]{:S(2)}) copy-start(s32[1,1024]{1,0:T(1,128)} %order_ref.1) | copy-start | bytes 12292
  1.4 35.6 %copy-start.6 = (s32[32]{0:T(128)S(1)}, s32[32]{0:T(128)}, u32[]{:S(2)}) copy-start(s32[32]{0:T(128)} %rows_ref.1) | copy-start | bytes 388
  1.4 35.6 %copy-start.7 = (s32[32]{0:T(128)S(1)}, s32[32]{0:T(128)}, u32[]{:S(2)}) copy-start(s32[32]{0:T(128)} %cols_ref.1) | copy-start | bytes 388
  30.9 12.3 %all-to-all-start.1 = ((bf16[4,256,256]{2,1,0:T(8,128)(2,1)}), bf16[4,256,256]{2,1,0:T(8,128)(2,1)S(1)}, u32[]{:S(2)}, u32[]{:S(2)}) async-start(bf16[4,256,256]{2,1,0:T(8,128)(2,1)} %spread_kernel.3), calls=%async_computation.1 | async-start | bytes 1048576 | tf_op jit(solution)/shard_map/all_to_all | solution.py:193
  36.9 1.2 copy-start.4
  43.2 20.3 %copy-start = (bf16[256,256]{1,0:T(8,128)(2,1)S(1)}, bf16[256,256]{1,0:T(8,128)(2,1)}, u32[]{:S(2)}) copy-start(bf16[256,256]{1,0:T(8,128)(2,1)} %weight_ref.1) | copy-start | bytes 393220
  43.2 20.3 %copy-start.1 = (bf16[64,256]{1,0:T(8,128)(2,1)S(1)}, bf16[64,256]{1,0:T(8,128)(2,1)}, u32[]{:S(2)}) copy-start(bf16[64,256]{1,0:T(8,128)(2,1)} %cot_ref.1) | copy-start | bytes 98308
  43.2 20.3 %copy-start.3 = (f32[256]{0:T(256)S(1)}, f32[256]{0:T(256)}, u32[]{:S(2)}) copy-start(f32[256]{0:T(256)} %param.16) | copy-start | bytes 3076

commit v7 on v6

--- a/solution.py
+++ b/solution.py
@@ -112,9 +112,10 @@
     dsum = (dot_nt(grad, weight_ref[...]) * scale).astype(BF16)
     weight_term = lax.dot_general(agg, grad, TN, preferred_element_type=F32)
     bias_rows = bias_block(jnp.sum(grad.astype(F32), axis=0, keepdims=True))
-    weight_term = weight_term.astype(BF16)
     for j in range(n_col):
-        chunk = weight_term[16 * j : 16 * (j + 1), :]
+        chunk = jnp.concatenate(
+            [weight_term[8 * (h * n_col + j) : 8 * (h * n_col + j + 1), :] for h in range(HALVES)], axis=0
+        ).astype(BF16)
         send_ref[j, :rows, :] = dsum[:, :LANES]
         send_ref[j, rows : 2 * rows, :] = dsum[:, LANES:]
         send_ref[j, 2 * rows : 2 * rows + 16, :] = chunk[:, :LANES]
@@ -129,7 +130,10 @@
     extra = recv_ref[0, 2 * rows :, :].astype(F32)
     for j in range(1, n_col):
         extra += recv_ref[j, 2 * rows :, :].astype(F32)
-    chunk = extra[:32, :].astype(BF16)
+    chunks = [
+        jnp.concatenate([extra[8 * h : 8 * h + 8, :], extra[16 + 8 * h : 24 + 8 * h, :]], axis=0).astype(BF16)
+        for h in range(HALVES)
+    ]
     bias_rows = merged_bias(extra[32:, :])
     for j in range(n_col):
         grads_ref[j * rows : (j + 1) * rows, :LANES] = recv_ref[j, :rows, :]
@@ -141,8 +145,8 @@
             base = 2 * own * k
             send_ref[i, base : base + own, :] = sums[k * own : (k + 1) * own, :LANES]
             send_ref[i, base + own : base + 2 * own, :] = sums[k * own : (k + 1) * own, LANES:]
-        send_ref[i, 2 * own * FAR : 2 * own * FAR + 32, :] = chunk
-        send_ref[i, 2 * own * FAR + 32 :, :] = bias_rows
+        send_ref[i, 2 * own * FAR : 2 * own * FAR + 16, :] = chunks[i // NEAR]
+        send_ref[i, 2 * own * FAR + 16 :, :] = bias_rows
 
 
 def merged_bias(rows):
@@ -151,27 +155,27 @@
 
 
 def middle_kernel(recv_ref, send_ref):
-    part = (recv_ref.shape[1] - 40) // FAR
+    part = (recv_ref.shape[1] - 24) // FAR
     total = recv_ref[0].astype(F32)
     for i in range(1, recv_ref.shape[0]):
         total += recv_ref[i].astype(F32)
     base = part * FAR
-    chunk = total[base : base + 32, :].astype(BF16)
-    bias_rows = merged_bias(total[base + 32 :, :])
+    chunk = total[base : base + 16, :].astype(BF16)
+    bias_rows = merged_bias(total[base + 16 :, :])
     for k in range(FAR):
         send_ref[k, :part, :] = total[k * part : (k + 1) * part, :].astype(BF16)
-        send_ref[k, part : part + 32, :] = chunk
-        send_ref[k, part + 32 :, :] = bias_rows
+        send_ref[k, part : part + 16, :] = chunk
+        send_ref[k, part + 16 :, :] = bias_rows
 
 
 def weight_kernel(recv_ref, spread_ref):
-    base = recv_ref.shape[1] - 40
-    total = recv_ref[0, base : base + 32, :].astype(F32)
+    base = recv_ref.shape[1] - 24
+    total = recv_ref[0, base : base + 16, :].astype(F32)
     for i in range(1, recv_ref.shape[0]):
-        total += recv_ref[i, base : base + 32, :].astype(F32)
+        total += recv_ref[i, base : base + 16, :].astype(F32)
     for i in range(spread_ref.shape[0]):
-        spread_ref[i, :, :LANES] = total[:16, :]
-        spread_ref[i, :, LANES:] = total[16:, :]
+        spread_ref[i, :, :LANES] = total[:8, :]
+        spread_ref[i, :, LANES:] = total[8:, :]
 
 
 def store_kernel(recv_ref, chunks_ref, output_ref, feature_ref, bias_ref, weight_ref, out_ref):
@@ -181,7 +185,7 @@
         total += recv_ref[i].astype(F32)
     feature_ref[:, :LANES] = total[:own, :].astype(BF16)
     feature_ref[:, LANES:] = total[own : 2 * own, :].astype(BF16)
-    base = 2 * own + 32
+    base = 2 * own + 16
     bias = total[base : base + 2, :] + total[base + 2 : base + 4, :]
     bias_ref[:, :LANES] = bias[:1, :]
     bias_ref[:, LANES:] = bias[1:, :]
@@ -250,15 +254,15 @@
         recv_grads = exchange(send_grads, "col")
         send_back = call(
             backward_kernel,
-            shape((n_near, 2 * own * FAR + 40, LANES), BF16),
+            shape((n_near, 2 * own * FAR + 24, LANES), BF16),
             [VMEM] * 2,
             [pltpu.VMEM((size, width), BF16)],
         )(matrix, recv_grads)
         recv_near = exchange(send_back, near_axes)
-        send_far = call(middle_kernel, shape((FAR, 2 * own + 40, LANES), BF16), [VMEM])(recv_near)
+        send_far = call(middle_kernel, shape((FAR, 2 * own + 24, LANES), BF16), [VMEM])(recv_near)
         recv_back = exchange(send_far, "far")
-        send_weight = call(weight_kernel, shape((n_col, 16, width), F32), [VMEM])(recv_back)
-        chunks = exchange(send_weight, "col")
+        send_weight = call(weight_kernel, shape((HALVES * n_col, 8, width), F32), [VMEM])(recv_back)
+        chunks = exchange(send_weight, ("half", "col"))
         feature_grad, bias_grad, weight_grad, output = call(
             store_kernel,
             (

time: 127 us -> 127 us (level)
  no operation moved by 1% of the time
where the time goes in v7:
time: 127 us
  blocking collectives  109 us (86%)
  Pallas kernels  7.3 us (6%)
  starting transfers between devices  5.37 us (4%)
  local copies, waits for them, and re-layouts  1.95 us (2%)
  between operations  1.37 us (1%)
  waiting for transfers between devices  1.31 us (1%)
    all_to_all x6, blocking collectives, exchange(): return lax.all_to_all(blocks, axes, split_axis=0, concat_axis=0, tiled=True)  109 us
    all_to_all x1, starting transfers between devices, exchange(): return lax.all_to_all(blocks, axes, split_axis=0, concat_axis=0, tiled=True)  5.37 us
    pallas_call x1, Pallas kernels, body(): call(edges_kernel, (shape((size, size), BF16), shape((8, n_col * LANES),...  3.71 us
  transfers between devices with their start and end apart: 1, of which 1 were waited for; matrix products, arithmetic and copies ran while one was open for 0% of the time, Pallas kernels for 3%

profile of v7, /device:TPU:1, one launch (start us, length us, event | category | flops | bytes accessed | tf_op | source)
XLA Modules:
  0.0 126.6 jit_solution(11336269330076079643)
XLA Ops:
  0.6 0.0 copy-start.2
  0.6 0.7 copy-done.2
  1.4 0.0 copy-start.5
  1.4 0.0 copy-start.6
  1.4 0.0 copy-start.7
  1.4 28.7 %all_to_all.35.block_ref = bf16[8,32,256]{2,1,0:T(8,128)(2,1)S(1)} all-to-all(bf16[8,32,256]{2,1,0:T(8,128)(2,1)S(1)} %spread_kernel.2), channel_id=1, replica_groups=mesh['half'=2,'far'=8,'near'=2,'col'=16] {'far'}, dimensions={0} | all-to-all | bytes 262144 | tf_op jit(solution)/shard_map/all_to_all | solution.py:197
  30.0 0.8 spread_kernel.3
  30.9 5.4 %all-to-all-start.1 = ((bf16[4,256,256]{2,1,0:T(8,128)(2,1)}), bf16[4,256,256]{2,1,0:T(8,128)(2,1)S(1)}, u32[]{:S(2)}, u32[]{:S(2)}) async-start(bf16[4,256,256]{2,1,0:T(8,128)(2,1)} %spread_kernel.3), calls=%async_computation.1 | async-start | bytes 1048576 | tf_op jit(solution)/shard_map/all_to_all | solution.py:197
  36.9 0.0 copy-done.5
  36.9 0.0 copy-done.6
  36.9 0.0 copy-done.7
  36.9 0.0 copy-start.4
  37.0 1.2 copy-done.4
  38.2 3.7 %edges_kernel.1 = (bf16[1024,1024]{1,0:T(8,128)(2,1)S(1)}, bf16[8,2048]{1,0:T(8,128)(2,1)S(1)}) custom-call(s32[1]{0:T(128)S(6)} %copy.13.count_ref, s32[32]{0:T(128)S(1)} %copy-done.6, s32[32]{0:T(128)S(1)} %copy-done.7, s32[1,1024]{1,0:T(1,128)S(1)} %copy-done.5, bf16[32,128,128]{2,1,0:T(8,128)(2,1)S(1)} %copy-done.4), custom_call_target="tpu_custom_call" | custom-call | flops 4294967296 | bytes 3145728 | tf_op jit(solution)/shard_map/edges_kernel/pallas_call | solution.py:235
  41.9 1.3 %all-to-all-done.1 = bf16[4,256,256]{2,1,0:T(8,128)(2,1)S(1)} async-done(((bf16[4,256,256]{2,1,0:T(8,128)(2,1)}), bf16[4,256,256]{2,1,0:T(8,128)(2,1)S(1)}, u32[]{:S(2)}, u32[]{:S(2)}) %all-to-all-start.1) | async-done | bytes 524320 | tf_op jit(solution)/shard_map/all_to_all | solution.py:197
  43.2 0.0 copy-start
  43.2 0.0 copy-start.1
  43.2 0.0 copy-start.3
  43.2 0.7 forward_kernel.1
  43.9 19.6 %all_to_all.36.recv_ref = bf16[16,136,128]{2,1,0:T(8,128)(2,1)S(1)} all-to-all(bf16[16,136,128]{2,1,0:T(8,128)(2,1)S(1)} %forward_kernel.1), channel_id=1, replica_groups=mesh['half'=2,'far'=8,'near'=2,'col'=16] {'col'}, dimensions={0} | all-to-all | bytes 1114112 | tf_op jit(solution)/shard_map/all_to_all | solution.py:197
  63.5 0.0 copy-done
  63.5 0.0 copy-done.1
  63.5 0.0 copy-done.3
  63.5 0.4 dense_kernel.1
  64.0 14.9 %all_to_all.37.recv_ref = bf16[16,168,128]{2,1,0:T(8,128)(2,1)S(1)} all-to-all(bf16[16,168,128]{2,1,0:T(8,128)(2,1)S(1)} %get-tuple-element.14), channel_id=1, replica_groups=mesh['half'=2,'far'=8,'near'=2,'col'=16] {'col'}, dimensions={0} | all-to-all | bytes 1376256 | tf_op jit(solution)/shard_map/all_to_all | solution.py:197
  78.8 0.8 backward_kernel.1
  79.6 13.3 %all_to_all.38.recv_ref = bf16[4,536,128]{2,1,0:T(8,128)(2,1)S(1)} all-to-all(bf16[4,536,128]{2,1,0:T(8,128)(2,1)S(1)} %backward_kernel.1), channel_id=1, replica_groups=mesh['half'=2,'far'=8,'near'=2,'col'=16] {'half','near'}, dimensions={0} | all-to-all | bytes 1097728 | tf_op jit(solution)/shard_map/all_to_all | solution.py:197
  92.9 0.1 middle_kernel.1
  93.0 17.1 %all_to_all.39.recv_ref = bf16[8,88,128]{2,1,0:T(8,128)(2,1)S(1)} all-to-all(bf16[8,88,128]{2,1,0:T(8,128)(2,1)S(1)} %middle_kernel.1), channel_id=1, replica_groups=mesh['half'=2,'far'=8,'near'=2,'col'=16] {'far'}, dimensions={0} | all-to-all | bytes 360448 | tf_op jit(solution)/shard_map/all_to_all | solution.py:197
  110.2 15.7 %all_to_all.40.chunks_ref = f32[32,8,256]{2,1,0:T(8,128)S(1)} all-to-all(f32[32,8,256]{2,1,0:T(8,128)S(1)} %weight_kernel.1), channel_id=1, replica_groups=mesh['half'=2,'far'=8,'near'=2,'col'=16] {'half','col'}, dimensions={0} | all-to-all | bytes 524288 | tf_op jit(solution)/shard_map/all_to_all | solution.py:197
  125.9 0.7 store_kernel.1
  (2 shorter events, 0.0 us)
Async XLA Ops:
  0.6 0.7 copy-start.2
  1.4 35.6 %copy-start.5 = (s32[1,1024]{1,0:T(1,128)S(1)}, s32[1,1024]{1,0:T(1,128)}, u32[]{:S(2)}) copy-start(s32[1,1024]{1,0:T(1,128)} %order_ref.1) | copy-start | bytes 12292
  1.4 35.6 %copy-start.6 = (s32[32]{0:T(128)S(1)}, s32[32]{0:T(128)}, u32[]{:S(2)}) copy-start(s32[32]{0:T(128)} %rows_ref.1) | copy-start | bytes 388
  1.4 35.6 %copy-start.7 = (s32[32]{0:T(128)S(1)}, s32[32]{0:T(128)}, u32[]{:S(2)}) copy-start(s32[32]{0:T(128)} %cols_ref.1) | copy-start | bytes 388
  30.9 12.3 %all-to-all-start.1 = ((bf16[4,256,256]{2,1,0:T(8,128)(2,1)}), bf16[4,256,256]{2,1,0:T(8,128)(2,1)S(1)}, u32[]{:S(2)}, u32[]{:S(2)}) async-start(bf16[4,256,256]{2,1,0:T(8,128)(2,1)} %spread_kernel.3), calls=%async_computation.1 | async-start | bytes 1048576 | tf_op jit(solution)/shard_map/all_to_all | solution.py:197
  36.9 1.2 copy-start.4
  43.2 20.3 %copy-start = (bf16[256,256]{1,0:T(8,128)(2,1)S(1)}, bf16[256,256]{1,0:T(8,128)(2,1)}, u32[]{:S(2)}) copy-start(bf16[256,256]{1,0:T(8,128)(2,1)} %weight_ref.1) | copy-start | bytes 393220
  43.2 20.3 %copy-start.1 = (bf16[64,256]{1,0:T(8,128)(2,1)S(1)}, bf16[64,256]{1,0:T(8,128)(2,1)}, u32[]{:S(2)}) copy-start(bf16[64,256]{1,0:T(8,128)(2,1)} %cot_ref.1) | copy-start | bytes 98308
  43.2 20.3 %copy-start.3 = (f32[256]{0:T(256)S(1)}, f32[256]{0:T(256)}, u32[]{:S(2)}) copy-start(f32[256]{0:T(256)} %param.16) | copy-start | bytes 3076
